TPU v7x, 32 devices: a whole 2x2x4 slice. The times are simulated.
32 devices in a mesh: mem: 4 (over y, x), seqi: 2 (over core), seqo: 4 (over z).
Axes of the slice: x: 2, y: 2, z: 4, core: 2. Of those that a mesh axis runs over, the one named last changes fastest.
Arguments:
- queries: bfloat16 [8, 512, 2048], P(('seqi', 'seqo'), 'mem'), may hold values from -6 to 6
- keys: bfloat16 [8, 512, 2048], P(('seqi', 'seqo'), 'mem'), may hold values from -6 to 6
- values: bfloat16 [8, 512, 2048], P(('seqi', 'seqo'), 'mem'), may hold values from -6 to 6
- log_decay: bfloat16 [16, 8, 512], P(None, ('seqi', 'seqo'), 'mem'), may hold values from -1 to 0
- routes: int32 [8, 512, 2], P(('seqi', 'seqo'), 'mem'), may hold values from 0 to 3, all different within a row; in each aligned block of 128 rows (0 to 127, 128 to 255, ..., all dimensions but the last counted through in order) at most 80 rows name the same one
- route_logits: bfloat16 [8, 512, 2], P(('seqi', 'seqo'), 'mem'), may hold values from -6 to 6
- cotangent: bfloat16 [8, 512, 2048], P(('seqi', 'seqo'), 'mem'), may hold values from -6 to 6
Outputs:
- output: bfloat16 [8, 512, 2048], P(('seqi', 'seqo'), 'mem')
- grad_queries: bfloat16 [8, 512, 2048], P(('seqi', 'seqo'), 'mem')
- grad_keys: bfloat16 [8, 512, 2048], P(('seqi', 'seqo'), 'mem')
- grad_values: bfloat16 [8, 512, 2048], P(('seqi', 'seqo'), 'mem')
Inputs may be any that keep to these rules, and one draw needn't show every extreme that they name: `routes`: in the rows of one device no memory is named by more than 80 rows, and in every draw some device names some memory exactly 80 times.
All inputs are finite; a program needn't handle non-finite values.
Results may differ from a plain program's by a relative error of at most 0.014.
Values may be sent and summed in bfloat16 or wider, within the bound.
A program may use at most 448 MiB of HBM per device.

v0:
```python
import math

import jax
import jax.numpy as jnp
from jax import lax
from jax.sharding import PartitionSpec as P

H = 16
DK = 128
MEM_DEV = 1
SHARD_STEPS = 128
CAP = 80


HIGH = lax.Precision.HIGH


def entering(value, axis, join, neutral, backward):
    count, mine = (lax.axis_size(axis), lax.axis_index(axis))
    pieces = jax.tree.map(lambda part: lax.all_gather(part, axis), value)
    if backward:
        pieces = jax.tree.map(lambda part: part[::-1], pieces)
        mine = count - 1 - mine
    total = jax.tree.map(
        lambda part, zero: jnp.full_like(part, 0) + jnp.asarray(zero, part.dtype), value, neutral
    )

    def hop(position, total):
        longer = join(total, jax.tree.map(lambda part: part[position], pieces))
        return jax.tree.map(lambda new, old: jnp.where(position < mine, new, old), longer, total)

    return lax.fori_loop(0, count - 1, hop, total)


def combine(earlier, later):
    return (earlier[0] * later[0], later[0][:, None, None] * earlier[1] + later[1])


def neutral(element):
    return (jnp.ones_like(element[0]), jnp.zeros_like(element[1]))


def seq_prefix(element, backward):
    return entering(element, ("seqi", "seqo"), combine, neutral(element), backward)


def as_blocks(array, count, span):
    return array.reshape((array.shape[0], count, span) + array.shape[2:])


def local_pass(raw_reads, factor, raw_writes, raw_values, log_rates):
    storage_channels, length, width = raw_reads.shape
    span = math.gcd(length, 128)
    count = length // span
    row_factor = jnp.broadcast_to(factor, (storage_channels, length, 1))
    reads = raw_reads.astype(jnp.float32) * row_factor
    writes = raw_writes.astype(jnp.float32)
    values_in = raw_values.astype(jnp.float32)
    cumulative = jnp.cumsum(log_rates, axis=1)
    inner = jnp.cumsum(log_rates.reshape(storage_channels, count, span), axis=2)
    lower = jnp.arange(span)[:, None] >= jnp.arange(span)[None, :]
    spread = inner[:, :, :, None] - inner[:, :, None, :]
    decay_matrix = jnp.where(lower, jnp.exp(jnp.where(lower, spread, 0.0)), 0.0)
    raw_scores = jnp.einsum(
        "nctd,ncsd->ncts",
        as_blocks(raw_reads, count, span),
        as_blocks(raw_writes, count, span),
        preferred_element_type=jnp.float32,
    )
    scores = raw_scores * as_blocks(row_factor, count, span) * decay_matrix
    within = jnp.einsum(
        "ncts,ncse->ncte", scores, as_blocks(values_in, count, span), precision=HIGH
    )
    inner_tail = jnp.exp(inner[:, :, -1:] - inner)
    stretch_decay = jnp.exp(inner[:, :, -1])
    stretch_state = jnp.einsum(
        "ncsd,ncse->ncde",
        as_blocks(writes, count, span) * inner_tail[..., None],
        as_blocks(values_in, count, span),
        precision=HIGH,
    )

    def advance(state, item):
        decay, addend = item
        return (decay[:, None, None] * state + addend, state)

    start = jnp.zeros((storage_channels, width, width), jnp.float32)
    unused, starts = lax.scan(
        advance, start, (stretch_decay.T, stretch_state.transpose(1, 0, 2, 3))
    )
    stretch_prefix = starts.transpose(1, 0, 2, 3)
    within = within + jnp.einsum(
        "nctd,ncde->ncte",
        as_blocks(reads, count, span) * jnp.exp(inner)[..., None],
        stretch_prefix,
        precision=HIGH,
    )
    within = within.reshape(storage_channels, length, width)
    tail_decay = jnp.exp(cumulative[:, -1:] - cumulative)
    total_decay = jnp.exp(cumulative[:, -1])
    state = jnp.einsum("nsd,nse->nde", writes * tail_decay[:, :, None], values_in, precision=HIGH)
    return (
        cumulative,
        decay_matrix,
        scores,
        within,
        tail_decay,
        total_decay,
        state,
        inner,
        stretch_prefix,
        stretch_decay,
        reads,
        writes,
        values_in,
        inner_tail,
    )


def carried(reads, cumulative, prefix):
    return jnp.einsum(
        "ntd,nde->nte", reads * jnp.exp(cumulative)[:, :, None], prefix, precision=HIGH
    )


def read_carry(reads, cumulative, cotan):
    return jnp.einsum(
        "ntd,nte->nde",
        reads * jnp.exp(cumulative)[:, :, None],
        cotan.astype(jnp.float32),
        precision=HIGH,
    )


def local_backward(raw_values, raw_cotan, passed, prefix, grad_state):
    (
        cumulative,
        decay_matrix,
        scores,
        within,
        tail_decay,
        total_decay,
        state,
        inner,
        stretch_prefix,
        stretch_decay,
        reads,
        writes,
        values_in,
        inner_tail,
    ) = passed
    storage_channels, length, width = reads.shape
    count = inner.shape[1]
    span = inner.shape[2]
    cotan = raw_cotan.astype(jnp.float32)
    cotan_blocks = as_blocks(cotan, count, span)
    read_blocks = as_blocks(reads, count, span)
    write_blocks = as_blocks(writes, count, span)
    value_blocks = as_blocks(values_in, count, span)
    masked = (
        jnp.einsum(
            "ncte,ncse->ncts",
            as_blocks(raw_cotan, count, span),
            as_blocks(raw_values, count, span),
            preferred_element_type=jnp.float32,
        )
        * decay_matrix
    )
    stretch_reads = jnp.einsum(
        "nctd,ncte->ncde", read_blocks * jnp.exp(inner)[..., None], cotan_blocks, precision=HIGH
    )

    def retreat(carry, item):
        decay, addend = item
        return (decay[:, None, None] * carry + addend, carry)

    start = jnp.zeros((storage_channels, width, width), jnp.float32)
    unused, later = lax.scan(
        retreat, start, (stretch_decay.T, stretch_reads.transpose(1, 0, 2, 3)), reverse=True
    )
    later_grad = later.transpose(1, 0, 2, 3)
    grad_reads = (
        jnp.einsum("ncts,ncsd->nctd", masked, write_blocks, precision=HIGH)
        + jnp.einsum("ncte,ncde->nctd", cotan_blocks, stretch_prefix, precision=HIGH)
        * jnp.exp(inner)[..., None]
    )
    grad_writes = (
        jnp.einsum("ncts,nctd->ncsd", masked, read_blocks, precision=HIGH)
        + jnp.einsum("ncse,ncde->ncsd", value_blocks, later_grad, precision=HIGH)
        * inner_tail[..., None]
    )
    grad_values = (
        jnp.einsum("ncts,ncte->ncse", scores, cotan_blocks, precision=HIGH)
        + jnp.einsum("ncsd,ncde->ncse", write_blocks, later_grad, precision=HIGH)
        * inner_tail[..., None]
    )
    grad_reads = (
        grad_reads.reshape(storage_channels, length, width)
        + jnp.einsum("nte,nde->ntd", cotan, prefix, precision=HIGH)
        * jnp.exp(cumulative)[:, :, None]
    )
    grad_writes = (
        grad_writes.reshape(storage_channels, length, width)
        + jnp.einsum("nse,nde->nsd", values_in, grad_state, precision=HIGH) * tail_decay[:, :, None]
    )
    grad_values = (
        grad_values.reshape(storage_channels, length, width)
        + jnp.einsum("nsd,nde->nse", writes, grad_state, precision=HIGH) * tail_decay[:, :, None]
    )
    return (grad_reads, grad_writes, grad_values)


def route_streams(block, head_count):
    groups, held, slots, features = block.shape
    head_size = features // head_count
    split = block.reshape(groups, held, slots, head_count, head_size).transpose(1, 3, 0, 2, 4)
    return split.reshape(held, head_count, groups * slots, head_size)


def route_rows(stream, groups):
    held, head_count, length, head_size = stream.shape
    slots = length // groups
    moved = stream.reshape(held, head_count, groups, slots, head_size).transpose(2, 0, 3, 1, 4)
    return moved.reshape(groups, held, slots, head_count * head_size)


def body(queries, keys, values, log_decay, routes, route_logits, cotangent):
    groups = lax.axis_size("mem")
    memories = MEM_DEV * groups
    features = H * DK
    total_tokens = SHARD_STEPS * groups * lax.axis_size("seqi") * lax.axis_size("seqo")
    scale = 2.0 / math.sqrt(DK * total_tokens)
    query_rows = queries[0]
    key_rows = keys[0]
    value_rows = values[0]
    cotan_rows = cotangent[0]
    gates = log_decay[:, 0, :]
    chosen = routes[0]
    logits = route_logits[0].astype(jnp.float32)
    first_weight = jax.nn.sigmoid(logits[:, 0] - logits[:, 1]).astype(jnp.bfloat16)
    second_weight = jax.nn.sigmoid(logits[:, 1] - logits[:, 0]).astype(jnp.bfloat16)
    member = chosen.reshape(-1)
    onehot = (member[:, None] == jnp.arange(memories, dtype=jnp.int32)[None, :]).astype(jnp.int32)
    earlier = jnp.cumsum(onehot, axis=0) - onehot
    position = jnp.sum(earlier * onehot, axis=1)
    slot_index = member * CAP + position
    owner_token = jnp.arange(2 * SHARD_STEPS, dtype=jnp.int32) // 2
    slot_table = jnp.full((memories * CAP,), SHARD_STEPS, jnp.int32).at[slot_index].set(owner_token)
    slot_weight = (
        jnp.zeros((memories * CAP,), jnp.bfloat16)
        .at[slot_index]
        .set(jnp.stack([first_weight, second_weight], 1).reshape(-1))
    )
    stacked = jnp.concatenate(
        [
            jnp.stack([query_rows, key_rows, value_rows], 1),
            jnp.zeros((1, 3, features), jnp.bfloat16),
        ],
        0,
    )
    packed = stacked[slot_table].reshape(groups, MEM_DEV, CAP, 3, features)
    gate_table = jnp.concatenate([gates.T, jnp.zeros((1, H), jnp.bfloat16)], 0)
    gate_rows = gate_table[slot_table].reshape(groups, MEM_DEV, CAP, H)
    weight_rows = slot_weight.reshape(groups, MEM_DEV, CAP)
    arrived, arrived_gates, arrived_weights = (
        lax.all_to_all(packed, "mem", split_axis=0, concat_axis=0, tiled=True),
        lax.all_to_all(gate_rows, "mem", split_axis=0, concat_axis=0, tiled=True),
        lax.all_to_all(weight_rows, "mem", split_axis=0, concat_axis=0, tiled=True),
    )
    length = groups * CAP
    routed_count = MEM_DEV * H
    factor = (
        arrived_weights.astype(jnp.float32).transpose(1, 0, 2).reshape(MEM_DEV, 1, length, 1)
        * scale
    )
    routed_factor = jnp.broadcast_to(factor, (MEM_DEV, H, length, 1)).reshape(
        routed_count, length, 1
    )
    routed_raw_reads = route_streams(arrived[:, :, :, 0], H).reshape(routed_count, length, DK)
    routed_raw_writes = route_streams(arrived[:, :, :, 1], H).reshape(routed_count, length, DK)
    routed_raw_values = route_streams(arrived[:, :, :, 2], H).reshape(routed_count, length, DK)
    routed_logs = (
        arrived_gates.astype(jnp.float32).transpose(1, 3, 0, 2).reshape(routed_count, length)
    )
    per_device = H // groups
    parted = jnp.stack(
        [
            query_rows.reshape(SHARD_STEPS, groups, per_device * DK),
            key_rows.reshape(SHARD_STEPS, groups, per_device * DK),
            value_rows.reshape(SHARD_STEPS, groups, per_device * DK),
        ],
        2,
    )
    gate_part = gates.T.reshape(SHARD_STEPS, groups, per_device)
    shared_in, shared_gates = (
        lax.all_to_all(parted, "mem", split_axis=1, concat_axis=0, tiled=True),
        lax.all_to_all(gate_part, "mem", split_axis=1, concat_axis=0, tiled=True),
    )
    shared_streams = (
        shared_in[:, 0].reshape(groups * SHARD_STEPS, 3, per_device, DK).transpose(1, 2, 0, 3)
    )
    shared_logs = shared_gates[:, 0].astype(jnp.float32).T
    shared_factor = jnp.full((1, 1, 1), scale, jnp.float32)
    routed_pass = local_pass(
        routed_raw_reads, routed_factor, routed_raw_writes, routed_raw_values, routed_logs
    )
    shared_pass = local_pass(
        shared_streams[0], shared_factor, shared_streams[1], shared_streams[2], shared_logs
    )
    shared_element = (shared_pass[5], shared_pass[6])
    joint = (
        jnp.concatenate([routed_pass[5], shared_element[0]], 0),
        jnp.concatenate([routed_pass[6], shared_element[1]], 0),
    )
    before_all = seq_prefix(joint, False)
    routed_prefix = before_all[1][:routed_count]
    shared_seq = (before_all[0][routed_count:], before_all[1][routed_count:])
    shared_prefix = shared_seq[1]
    routed_out = routed_pass[3] + carried(routed_pass[10], routed_pass[0], routed_prefix)
    routed_half = routed_out.astype(jnp.bfloat16).reshape(MEM_DEV, H, length, DK)
    returned = lax.all_to_all(
        route_rows(routed_half, groups), "mem", split_axis=0, concat_axis=0, tiled=True
    )
    routed_sum = (
        returned.reshape(memories * CAP, features)[slot_index]
        .reshape(SHARD_STEPS, 2, features)
        .astype(jnp.float32)
        .sum(1)
    )
    shared_out = (shared_pass[3] + carried(shared_pass[10], shared_pass[0], shared_prefix)).astype(
        jnp.bfloat16
    )
    outgoing = shared_out.transpose(1, 0, 2).reshape(groups * SHARD_STEPS, 1, per_device * DK)
    shared_back = lax.all_to_all(outgoing, "mem", split_axis=0, concat_axis=1, tiled=True).reshape(
        SHARD_STEPS, features
    )
    output = (routed_sum + shared_back.astype(jnp.float32)).astype(jnp.bfloat16)
    cotan_table = jnp.concatenate([cotan_rows, jnp.zeros((1, features), jnp.bfloat16)], 0)
    cotan_slots = cotan_table[slot_table].reshape(groups, MEM_DEV, CAP, features)
    arrived_cotan = lax.all_to_all(cotan_slots, "mem", split_axis=0, concat_axis=0, tiled=True)
    routed_cotan = route_streams(arrived_cotan, H).reshape(routed_count, length, DK)
    shared_cotan_in = lax.all_to_all(
        cotan_rows.reshape(SHARD_STEPS, groups, per_device * DK),
        "mem",
        split_axis=1,
        concat_axis=0,
        tiled=True,
    )
    shared_cotan = (
        shared_cotan_in[:, 0].reshape(groups * SHARD_STEPS, per_device, DK).transpose(1, 0, 2)
    )
    routed_carry = read_carry(routed_pass[10], routed_pass[0], routed_cotan)
    shared_carry = read_carry(shared_pass[10], shared_pass[0], shared_cotan)
    shared_grad_element = (shared_pass[5], shared_carry)
    joint_grad = (
        jnp.concatenate([routed_pass[5], shared_grad_element[0]], 0),
        jnp.concatenate([routed_carry, shared_grad_element[1]], 0),
    )
    after_all = seq_prefix(joint_grad, True)
    routed_grad_state = after_all[1][:routed_count]
    shared_after = (after_all[0][routed_count:], after_all[1][routed_count:])
    shared_grad_state = shared_after[1]
    routed_grads = local_backward(
        routed_raw_values, routed_cotan, routed_pass, routed_prefix, routed_grad_state
    )
    grad_query_slots = routed_grads[0].reshape(MEM_DEV, H, length, DK) * factor
    grad_key_slots = routed_grads[1].reshape(MEM_DEV, H, length, DK)
    grad_value_slots = routed_grads[2].reshape(MEM_DEV, H, length, DK)
    grad_stack = jnp.stack(
        [
            route_rows(grad_query_slots.astype(jnp.bfloat16), groups),
            route_rows(grad_key_slots.astype(jnp.bfloat16), groups),
            route_rows(grad_value_slots.astype(jnp.bfloat16), groups),
        ],
        3,
    )
    returned_grads = lax.all_to_all(grad_stack, "mem", split_axis=0, concat_axis=0, tiled=True)
    routed_grad_sum = (
        returned_grads.reshape(memories * CAP, 3, features)[slot_index]
        .reshape(SHARD_STEPS, 2, 3, features)
        .astype(jnp.float32)
        .sum(1)
    )
    shared_grads = local_backward(
        shared_streams[2], shared_cotan, shared_pass, shared_prefix, shared_grad_state
    )
    shared_stack = jnp.stack(
        [
            (shared_grads[0] * scale).astype(jnp.bfloat16),
            shared_grads[1].astype(jnp.bfloat16),
            shared_grads[2].astype(jnp.bfloat16),
        ],
        0,
    )
    outgoing_grads = shared_stack.transpose(2, 0, 1, 3).reshape(
        groups * SHARD_STEPS, 3, 1, per_device * DK
    )
    shared_grad_back = lax.all_to_all(
        outgoing_grads, "mem", split_axis=0, concat_axis=2, tiled=True
    ).reshape(SHARD_STEPS, 3, features)
    grads_all = (routed_grad_sum + shared_grad_back.astype(jnp.float32)).astype(jnp.bfloat16)
    return (
        output.reshape(1, SHARD_STEPS, features),
        grads_all[:, 0].reshape(1, SHARD_STEPS, features),
        grads_all[:, 1].reshape(1, SHARD_STEPS, features),
        grads_all[:, 2].reshape(1, SHARD_STEPS, features),
    )


def solution(mesh):
    return jax.shard_map(
        body,
        mesh=mesh,
        in_specs=(
            P(("seqi", "seqo"), "mem", None),
            P(("seqi", "seqo"), "mem", None),
            P(("seqi", "seqo"), "mem", None),
            P(None, ("seqi", "seqo"), "mem"),
            P(("seqi", "seqo"), "mem", None),
            P(("seqi", "seqo"), "mem", None),
            P(("seqi", "seqo"), "mem", None),
        ),
        out_specs=(
            P(("seqi", "seqo"), "mem", None),
            P(("seqi", "seqo"), "mem", None),
            P(("seqi", "seqo"), "mem", None),
            P(("seqi", "seqo"), "mem", None),
        ),
        check_vma=False,
    )
```

profile of v0, /device:TPU:0, one launch (start us, length us, event | category | flops | bytes accessed | tf_op | source)
XLA Modules:
  0.0 551.6 jit_solution(16314193207405993574)
XLA Ops:
  14.7 5.2 all-to-all-start.1
  60.8 5.8 %all-to-all-done.7 = bf16[4,1,80,2048]{3,2,1,0:T(8,128)(2,1)S(1)} async-done(((bf16[4,1,80,2048]{3,2,1,0:T(8,128)(2,1)}), bf16[4,1,80,2048]{3,2,1,0:T(8,128)(2,1)S(1)}, u32[]{:S(2)}, u32[]{:S(2)}) %all-to-all-start.7) | async-done | bytes 1310752 | tf_op jit(solution)/shard_map/all_to_all | solution.py:340
  66.5 4.6 all-to-all-start.4
  77.4 13.2 %gather_fusion = bf16[320,3,2048]{2,1,0:T(4,128)(2,1)} fusion(bf16[129,3,2048]{2,1,0:T(4,128)(2,1)S(1)} %fusion.44, s32[1024]{0:T(1024)S(1)} %pad_clamp_fusion.1), kind=kCustom, calls=%fused_computation | custom fusion | bytes 7865600 | tf_op jit(solution)/shard_map/gather | solution.py:261
  90.6 7.2 %copy.285 = bf16[4,1,80,3,2048]{4,2,3,1,0:T(8,128)(2,1)} copy(bf16[4,1,80,3,2048]{4,3,2,0,1:T(4,128)(2,1)} %bitcast.467) | data formatting | bytes 7864320 | tf_op jit(solution)/shard_map/reshape | solution.py:261
  97.8 4.9 all-to-all-start
  118.9 23.9 %all-to-all-done = bf16[4,1,80,3,2048]{4,2,3,1,0:T(8,128)(2,1)} async-done(((bf16[4,1,80,3,2048]{4,2,3,1,0:T(8,128)(2,1)}), bf16[4,1,80,3,2048]{4,2,3,1,0:T(8,128)(2,1)}, u32[]{:S(2)}, u32[]{:S(2)}) %all-to-all-start) | async-done | bytes 3932192 | tf_op jit(solution)/shard_map/all_to_all | solution.py:266
  142.8 4.1 fusion.143
  157.7 18.6 %all-reduce.4 = f32[160]{0:T(256)S(1)} all-reduce(f32[160]{0:T(256)S(1)} %maximum_dynamic-update-slice_fusion), channel_id=2, replica_groups=mesh['mem'=4,'seqi'=2,'seqo'=4] {'seqi','seqo'}, use_global_device_ids=true, to_apply=%add.4 | all-reduce | flops 160 | bytes 1280
  196.7 15.7 %while.90 = (s32[]{:T(128)}, f32[4,128,128]{2,1,0:T(8,128)}, f32[4,4,128,128]{3,2,1,0:T(8,128)}, f32[4,4]{1,0:T(4,128)}, f32[4,4,128,128]{3,2,0,1:T(8,128)}, /*index=5*/s32[]{:T(128)}, s32[]{:T(128)}) while((s32[]{:T(128)}, f32[4,128,128]{2,1,0:T(8,128)}, f32[4,4,128,128]{3,2,1,0:T(8,128)}, f32[4,4]{1,0:T(4,128)}, ...), condition=%wide.region_16.17_spmd.clone, body=%wide.region_15.16_spmd.clone.sunk | while | flops 262147 | bytes 1311376 | solution.py:88
  229.9 15.9 %while.93 = (s32[]{:T(128)}, f32[4,128,128]{2,1,0:T(8,128)}, f32[4,4,128,128]{3,2,1,0:T(8,128)}, f32[4,4]{1,0:T(4,128)}, f32[4,4,128,128]{3,2,0,1:T(8,128)}, /*index=5*/s32[]{:T(128)}, s32[]{:T(128)}, s32[]{:T(128)}) while((s32[]{:T(128)}, f32[4,128,128]{2,1,0:T(8,128)}, f32[4,4,128,128]{3,2,1,0:T(8,128)}, f32[4,4]{1,0:T(4,128)}, ...), condition=%wide.region_23.24_spmd.clone, body=%wide.region_22.23_spmd.clone.sunk | while | flops 262148 | bytes 1310888 | solution.py:178
  261.1 4.3 fusion.28
  265.4 5.4 fusion.38
  270.8 5.4 fusion.35
  279.1 16.3 %while.91 = (s32[]{:T(128)}, f32[16,128,128]{2,1,0:T(8,128)S(1)}, f32[5,16,128,128]{3,2,1,0:T(8,128)}, f32[5,16]{1,0:T(8,128)}, f32[5,16,128,128]{3,2,0,1:T(8,128)}, /*index=5*/s32[]{:T(128)}, s32[]{:T(128)}, s32[]{:T(128)}) while((s32[]{:T(128)}, f32[16,128,128]{2,1,0:T(8,128)S(1)}, f32[5,16,128,128]{3,2,1,0:T(8,128)}, ...), condition=%wide.region_18.19_spmd.clone, body=%wide.region_17.18_spmd.clone.sunk | while | flops 1048580 | bytes 5243192 | solution.py:178
  295.5 6.1 %fusion.6 = f32[16,5,64,128]{3,2,1,0:T(8,128)} fusion(bf16[16,5,64,128]{3,2,1,0:T(8,128)(2,1)} %bitcast.460, f32[5,16,128,128]{3,2,1,0:T(8,128)} %get-tuple-element.455), kind=kOutput, calls=%fused_computation.30 | convolution fusion | flops 503316480 | bytes 9175040 | tf_op jit(solution)/shard_map/ncsd,ncde->ncse/dot_general | solution.py:194
  304.5 16.0 %while.88 = (s32[]{:T(128)}, f32[16,128,128]{2,1,0:T(8,128)S(1)}, f32[5,16,128,128]{3,2,1,0:T(8,128)}, f32[5,16]{1,0:T(8,128)}, f32[5,16,128,128]{3,2,0,1:T(8,128)}, /*index=5*/s32[]{:T(128)}, s32[]{:T(128)}) while((s32[]{:T(128)}, f32[16,128,128]{2,1,0:T(8,128)S(1)}, f32[5,16,128,128]{3,2,1,0:T(8,128)}, f32[5,16]{1,0:T(8,128)}, ...), condition=%wide.region_7.8_spmd.clone, body=%wide.region_6.7_spmd.clone.sunk | while | flops 1048579 | bytes 5243680 | solution.py:88
  320.5 5.5 fusion.12
  332.2 4.9 multiply_add_fusion.2
  337.1 4.8 multiply_add_fusion.1
  342.0 9.5 %rev.7 = f32[8,20,128,128]{3,2,1,0:T(8,128)} reverse(f32[8,20,128,128]{3,2,1,0:T(8,128)} %bitcast.482), dimensions={0} | reverse | bytes 20971520 | tf_op jit(solution)/shard_map/rev | solution.py:22
  353.0 16.4 %while.89 = (s32[]{:T(128)}, f32[20,128,128]{2,1,0:T(8,128)S(1)}, s32[]{:T(128)}, f32[8,20]{1,0:T(8,128)}, f32[8,20,128,128]{3,2,1,0:T(8,128)}, /*index=5*/s32[]{:T(128)}, s32[]{:T(128)}) while((s32[]{:T(128)}, f32[20,128,128]{2,1,0:T(8,128)S(1)}, s32[]{:T(128)}, f32[8,20]{1,0:T(8,128)}, f32[8,20,128,128]{3,2,1,0:T(8,128)}, ...), condition=%wide.region_13.14_spmd.clone, body=%wide.region_12.13_spmd.clone.sunk | while | flops 1310724 | bytes 3932505 | solution.py:32
  379.5 4.3 fusion.21
  391.6 25.5 %while.92 = (s32[]{:T(128)}, f32[20,128,128]{2,1,0:T(8,128)}, s32[]{:T(128)}, f32[8,20]{1,0:T(8,128)}, f32[8,20,128,128]{3,2,1,0:T(8,128)}, /*index=5*/s32[]{:T(128)}, s32[]{:T(128)}) while((s32[]{:T(128)}, f32[20,128,128]{2,1,0:T(8,128)}, s32[]{:T(128)}, f32[8,20]{1,0:T(8,128)}, f32[8,20,128,128]{3,2,1,0:T(8,128)}, ...), condition=%wide.region_20.21_spmd.clone, body=%wide.region_19.20_spmd.clone.sunk | while | flops 1310724 | bytes 3932505 | solution.py:32
  425.3 4.4 copy.358
  429.7 4.7 all-to-all-start.10
  461.6 5.1 all-to-all-start.9
  488.0 3.9 copy.361
  491.9 19.0 %all-to-all-done.9 = bf16[4,1,80,3,2048]{4,2,3,1,0:T(8,128)(2,1)} async-done(((bf16[4,1,80,3,2048]{4,2,3,1,0:T(8,128)(2,1)}), bf16[4,1,80,3,2048]{4,2,3,1,0:T(8,128)(2,1)}, u32[]{:S(2)}, u32[]{:S(2)}) %all-to-all-start.9) | async-done | bytes 3932192 | tf_op jit(solution)/shard_map/all_to_all | solution.py:377
  510.9 7.9 %copy.342 = bf16[4,1,80,3,2048]{4,3,2,0,1:T(4,128)(2,1)} copy(bf16[4,1,80,3,2048]{4,2,3,1,0:T(8,128)(2,1)} %all-to-all-done.9) | data formatting | bytes 7864320 | tf_op jit(solution)/shard_map/all_to_all | solution.py:377
  518.8 12.6 %gather_fusion.4 = bf16[256,3,2048]{2,1,0:T(4,128)(2,1)} fusion(bf16[320,3,2048]{2,1,0:T(4,128)(2,1)} %bitcast.472, s32[1024]{0:T(1024)S(1)} %pad_clamp_fusion), kind=kCustom, calls=%fused_computation.4 | custom fusion | bytes 6292480 | tf_op jit(solution)/shard_map/gather | solution.py:379
  531.4 6.3 %convert_reduce_fusion = f32[128,3,2048]{2,1,0:T(4,128)S(1)} fusion(bf16[256,3,2048]{2,1,0:T(4,128)(2,1)} %gather_fusion.4), kind=kLoop, calls=%fused_computation.29 | loop fusion | flops 2359296 | bytes 6291456 | tf_op jit(solution)/shard_map/reduce_sum | solution.py:382
  (439 shorter events, 332.6 us)
Async XLA Ops:
  7.2 36.6 %copy-start.47 = (bf16[1,128,2048]{2,1,0:T(8,128)(2,1)S(1)}, bf16[1,128,2048]{2,1,0:T(8,128)(2,1)}, u32[]{:S(2)}) copy-start(bf16[1,128,2048]{2,1,0:T(8,128)(2,1)} %param.25) | copy-start | bytes 1572868
  11.9 8.0 %copy-start.70 = (s32[256,1]{0,1:T(1,128)}, s32[256,1]{0,1:T(1,128)S(1)}, u32[]{:S(2)}) copy-start(s32[256,1]{0,1:T(1,128)S(1)} %compare_select_fusion) | copy-start | bytes 3076
  14.7 9.7 %all-to-all-start.1 = ((bf16[4,1,80]{2,1,0:T(2,128)(2,1)}), bf16[4,1,80]{2,1,0:T(2,128)(2,1)S(1)}, u32[]{:S(2)}, u32[]{:S(2)}) async-start(bf16[4,1,80]{2,1,0:T(2,128)(2,1)} %reshape.436), calls=%async_computation.1 | async-start | bytes 4096 | tf_op jit(solution)/shard_map/all_to_all | solution.py:268
  24.4 7.9 %all-to-all-start.3 = ((bf16[128,4,4]{0,2,1:T(4,128)(2,1)}), bf16[128,4,4]{0,2,1:T(4,128)(2,1)S(1)}, u32[]{:S(2)}, u32[]{:S(2)}) async-start(bf16[128,4,4]{0,2,1:T(4,128)(2,1)} %bitcast.535), calls=%async_computation.3 | async-start | bytes 8192 | tf_op jit(solution)/shard_map/all_to_all | solution.py:297
  32.3 7.9 %all-to-all-start.2 = ((bf16[4,1,80,16]{2,3,1,0:T(8,128)(2,1)}), bf16[4,1,80,16]{2,3,1,0:T(8,128)(2,1)S(1)}, u32[]{:S(2)}, u32[]{:S(2)}) async-start(bf16[4,1,80,16]{2,3,1,0:T(8,128)(2,1)} %copy.291), calls=%async_computation.2 | async-start | bytes 32768 | tf_op jit(solution)/shard_map/all_to_all | solution.py:267
  40.3 10.0 %all-to-all-start.8 = ((bf16[128,4,512]{2,0,1:T(8,128)(2,1)}), bf16[128,4,512]{2,0,1:T(8,128)(2,1)S(1)}, u32[]{:S(2)}, u32[]{:S(2)}) async-start(bf16[128,4,512]{2,0,1:T(8,128)(2,1)} %copy.334), calls=%async_computation.8 | async-start | bytes 1048576 | tf_op jit(solution)/shard_map/all_to_all | solution.py:342
  46.8 7.8 %copy-start.42 = (bf16[1,128,2048]{2,1,0:T(8,128)(2,1)S(1)}, bf16[1,128,2048]{2,1,0:T(8,128)(2,1)}, u32[]{:S(2)}) copy-start(bf16[1,128,2048]{2,1,0:T(8,128)(2,1)} %param.19) | copy-start | bytes 1572868
  46.8 8.8 %copy-start.43 = (bf16[1,128,2048]{2,1,0:T(8,128)(2,1)S(1)}, bf16[1,128,2048]{2,1,0:T(8,128)(2,1)}, u32[]{:S(2)}) copy-start(bf16[1,128,2048]{2,1,0:T(8,128)(2,1)} %param.20) | copy-start | bytes 1572868
  46.9 9.8 %copy-start.45 = (bf16[1,128,2048]{2,1,0:T(8,128)(2,1)S(1)}, bf16[1,128,2048]{2,1,0:T(8,128)(2,1)}, u32[]{:S(2)}) copy-start(bf16[1,128,2048]{2,1,0:T(8,128)(2,1)} %param.21) | copy-start | bytes 1572868
  51.1 15.4 %all-to-all-start.7 = ((bf16[4,1,80,2048]{3,2,1,0:T(8,128)(2,1)}), bf16[4,1,80,2048]{3,2,1,0:T(8,128)(2,1)S(1)}, u32[]{:S(2)}, u32[]{:S(2)}) async-start(bf16[4,1,80,2048]{3,2,1,0:T(8,128)(2,1)} %bitcast.64), calls=%async_computation.7 | async-start | bytes 2621440 | tf_op jit(solution)/shard_map/all_to_all | solution.py:340
  60.8 11.2 %copy-start.44 = (bf16[1,128,2048]{2,1,0:T(8,128)(2,1)S(1)}, bf16[1,128,2048]{2,1,0:T(8,128)(2,1)}, u32[]{:S(2)}) copy-start(bf16[1,128,2048]{2,1,0:T(8,128)(2,1)} %param.20) | copy-start | bytes 1572868
  60.8 12.1 %copy-start.46 = (bf16[1,128,2048]{2,1,0:T(8,128)(2,1)S(1)}, bf16[1,128,2048]{2,1,0:T(8,128)(2,1)}, u32[]{:S(2)}) copy-start(bf16[1,128,2048]{2,1,0:T(8,128)(2,1)} %param.21) | copy-start | bytes 1572868
  66.5 31.3 %all-to-all-start.4 = ((bf16[128,4,3,512]{3,0,2,1:T(8,128)(2,1)}), bf16[128,4,3,512]{3,0,2,1:T(8,128)(2,1)}, u32[]{:S(2)}, u32[]{:S(2)}) async-start(bf16[128,4,3,512]{3,0,2,1:T(8,128)(2,1)} %copy.312), calls=%async_computation.4 | async-start | bytes 3145728 | tf_op jit(solution)/shard_map/all_to_all | solution.py:296
  97.8 11.4 %copy-start.49 = (bf16[128,4,512]{2,0,1:T(8,128)(2,1)S(1)}, bf16[128,4,512]{2,0,1:T(8,128)(2,1)}, u32[]{:S(2)}) copy-start(bf16[128,4,512]{2,0,1:T(8,128)(2,1)} %copy-done.48) | copy-start | bytes 1572868
  97.8 45.0 %all-to-all-start = ((bf16[4,1,80,3,2048]{4,2,3,1,0:T(8,128)(2,1)}), bf16[4,1,80,3,2048]{4,2,3,1,0:T(8,128)(2,1)}, u32[]{:S(2)}, u32[]{:S(2)}) async-start(bf16[4,1,80,3,2048]{4,2,3,1,0:T(8,128)(2,1)} %copy.285), calls=%async_computation | async-start | bytes 7864320 | tf_op jit(solution)/shard_map/all_to_all | solution.py:266
  102.7 239.2 %all-gather.8.cloned.1.call-start = ((), (), s32[]{:S(2)}) async-start(), calls=%async_computation.12 | async-start | bytes 11796480 | tf_op jit(solution)/shard_map/all_gather | solution.py:20
  104.0 45.5 %copy-start.61 = (f32[320]{0:T(512)}, f32[320]{0:T(512)S(1)}, u32[]{:S(2)}) copy-start(f32[320]{0:T(512)S(1)} %mul.405) | copy-start | bytes 3844
  107.1 9.4 %copy-start.64 = (f32[4,512]{1,0:T(4,128)}, f32[4,512]{1,0:T(4,128)S(1)}, u32[]{:S(2)}) copy-start(f32[4,512]{1,0:T(4,128)S(1)} %get-tuple-element.745) | copy-start | bytes 24580
  109.2 40.3 %copy-start.53 = (f32[16,320]{1,0:T(8,128)}, f32[16,320]{1,0:T(8,128)S(1)}, u32[]{:S(2)}) copy-start(f32[16,320]{1,0:T(8,128)S(1)} %get-tuple-element.741) | copy-start | bytes 61444
  110.8 38.7 %copy-start.1 = (bf16[1,16,4,80,128]{4,3,2,1,0:T(8,128)(2,1)}, bf16[1,16,4,80,128]{4,3,2,1,0:T(8,128)(2,1)S(1)}, u32[]{:S(2)}) copy-start(bf16[1,16,4,80,128]{4,3,2,1,0:T(8,128)(2,1)S(1)} %copy.327) | copy-start | bytes 3932164
  153.4 199.6 %all-gather.6.cloned.1.call-start = ((), (), s32[]{:S(2)}) async-start(), calls=%async_computation.11 | async-start | bytes 11796480 | tf_op jit(solution)/shard_map/all_gather | solution.py:20
  196.7 15.7 %copy-start.57 = (f32[4,4,128]{2,1,0:T(4,128)S(1)}, f32[4,4,128]{2,1,0:T(4,128)}, u32[]{:S(2)}) copy-start(f32[4,4,128]{2,1,0:T(4,128)} %get-tuple-element.747) | copy-start | bytes 24580
  253.9 16.9 %copy-start.10 = (bf16[1,16,4,80,128]{4,3,2,1,0:T(8,128)(2,1)}, bf16[1,16,4,80,128]{4,3,2,1,0:T(8,128)(2,1)S(1)}, u32[]{:S(2)}) copy-start(bf16[1,16,4,80,128]{4,3,2,1,0:T(8,128)(2,1)S(1)} %copy.286) | copy-start | bytes 3932164
  320.5 11.7 %slice-start.2 = ((s8[5242880]{0:T(1024)(128)(4,1)}), s8[4194304]{0:T(1024)(128)(4,1)S(1)}, s32[]{:S(2)}) async-start(s8[5242880]{0:T(1024)(128)(4,1)} %bitcast.457), calls=%async_computation.15 | async-start | bytes 8388608
  328.7 8.4 %slice-start = ((s8[5242880]{0:T(1024)(128)(4,1)}), s8[4194304]{0:T(1024)(128)(4,1)S(1)}, s32[]{:S(2)}) async-start(s8[5242880]{0:T(1024)(128)(4,1)} %bitcast.455), calls=%async_computation.13 | async-start | bytes 8388608
  372.9 6.6 %copy-start.54 = (f32[16,320]{1,0:T(8,128)S(1)}, f32[16,320]{1,0:T(8,128)}, u32[]{:S(2)}) copy-start(f32[16,320]{1,0:T(8,128)} %copy-done.53) | copy-start | bytes 61444
  372.9 6.6 %copy-start.62 = (f32[320]{0:T(512)S(1)}, f32[320]{0:T(512)}, u32[]{:S(2)}) copy-start(f32[320]{0:T(512)} %copy-done.61) | copy-start | bytes 3844
  375.9 12.2 %all-to-all-start.6 = ((bf16[4,2,32768]{2,1,0:T(2,128)(2,1)}), bf16[4,2,32768]{2,1,0:T(2,128)(2,1)S(1)}, u32[]{:S(2)}, u32[]{:S(2)}) async-start(bf16[4,2,32768]{2,1,0:T(2,128)(2,1)} %reshape.455), calls=%async_computation.6 | async-start | bytes 1048576 | tf_op jit(solution)/shard_map/all_to_all | solution.py:334
  388.0 41.7 %all-to-all-start.5 = ((bf16[4,1,80,2048]{3,2,1,0:T(8,128)(2,1)}), bf16[4,1,80,2048]{3,2,1,0:T(8,128)(2,1)S(1)}, u32[]{:S(2)}, u32[]{:S(2)}) async-start(bf16[4,1,80,2048]{3,2,1,0:T(8,128)(2,1)} %bitcast.503), calls=%async_computation.5 | async-start | bytes 2621440 | tf_op jit(solution)/shard_map/all_to_all | solution.py:321
  391.6 25.6 %copy-start.56 = (f32[4,512]{1,0:T(4,128)S(1)}, f32[4,512]{1,0:T(4,128)}, u32[]{:S(2)}) copy-start(f32[4,512]{1,0:T(4,128)} %get-tuple-element.744) | copy-start | bytes 24580
  429.7 31.8 %all-to-all-start.10 = ((bf16[512,3,1,512]{3,1,2,0:T(4,128)(2,1)}), bf16[512,3,1,512]{3,1,2,0:T(4,128)(2,1)}, u32[]{:S(2)}, u32[]{:S(2)}) async-start(bf16[512,3,1,512]{3,1,2,0:T(4,128)(2,1)} %copy.358), calls=%async_computation.10 | async-start | bytes 4194304 | tf_op jit(solution)/shard_map/all_to_all | solution.py:398
  461.6 49.3 %all-to-all-start.9 = ((bf16[4,1,80,3,2048]{4,2,3,1,0:T(8,128)(2,1)}), bf16[4,1,80,3,2048]{4,2,3,1,0:T(8,128)(2,1)}, u32[]{:S(2)}, u32[]{:S(2)}) async-start(bf16[4,1,80,3,2048]{4,2,3,1,0:T(8,128)(2,1)} %copy.341), calls=%async_computation.9 | async-start | bytes 7864320 | tf_op jit(solution)/shard_map/all_to_all | solution.py:377
  (60 other events, 189.2 us)
Sparse Core Ops, SparseCore 0:
  153.5 100.0 all-gather.7
  255.2 97.7 all-gather.5
where the time goes:
time: 561 us; the launch traced here: 552 us
  local copies, waits for them, and re-layouts  181 us (32%)
  other arithmetic  123 us (22%)
  matrix products  103 us (18%)
  waiting for transfers between devices  62.8 us (11%)
  starting transfers between devices  45.8 us (8%)
  blocking collectives  18.6 us (3%)
  between operations  16.3 us (3%)
    select_n x14, other arithmetic, hop(): jnp.where(position < mine, new, old)  32 us
    all_to_all x1, waiting for transfers between devices, body(): lax.all_to_all(packed, 'mem', split_axis=0, concat_axis=0, tiled=True)  23.9 us
    dynamic_update_slice x18, other arithmetic, local_pass(): lax.scan(advance, start, (stretch_decay.T, stretch_state.transpose(1, 0,...  22.1 us
    all_to_all x1, waiting for transfers between devices, body(): lax.all_to_all(grad_stack, 'mem', split_axis=0, concat_axis=0, tiled=True)  19 us
    unnamed x177, local copies, waits for them, and re-layouts  18.9 us
    unnamed x1, blocking collectives  18.6 us
    add x9, other arithmetic, advance(): return (decay[:, None, None] * state + addend, state)  14.4 us
    add x9, other arithmetic, retreat(): return (decay[:, None, None] * carry + addend, carry)  14.4 us
  transfers between devices with their start and end apart: 13, of which 9 were waited for; matrix products, arithmetic and copies ran while one was open for 59% of the time, Pallas kernels for 0%

commit v1 on v0

v1 whole, which is shorter than its diff:
```python
import functools
import math

import jax
import jax.numpy as jnp
from jax import lax
from jax.experimental import pallas as pl
from jax.experimental.pallas import tpu as pltpu
from jax.sharding import PartitionSpec as P

DK = 128
MEM_DEV = 1
MESH = pl.DeviceIdType.MESH
F32 = jnp.float32
BF16 = jnp.bfloat16
PAD = 24


def dot(left, right, left_dim, right_dim):
    return lax.dot_general(
        left, right, (((left_dim,), (right_dim,)), ((), ())), preferred_element_type=F32
    )


def tables(gates, chosen, logits, groups, memories, scale):
    heads, span = gates.shape
    held = heads // groups
    first = jax.nn.sigmoid(logits[:, 0] - logits[:, 1]).astype(BF16).astype(F32)
    second = jax.nn.sigmoid(logits[:, 1] - logits[:, 0]).astype(BF16).astype(F32)
    names = jnp.arange(memories, dtype=jnp.int32)[:, None]
    hit_first = (chosen[:, 0][None, :] == names).astype(F32)
    hit_second = (chosen[:, 1][None, :] == names).astype(F32)
    ones = jnp.ones((1, span), F32)
    mask = jnp.concatenate([hit_first + hit_second, ones], 0)
    read = jnp.concatenate([first[None] * hit_first + second[None] * hit_second, ones], 0) * scale
    rates = gates[:, None, :] * mask[None]
    upper = (jnp.arange(span)[:, None] <= jnp.arange(span)[None, :]).astype(F32)
    total = jnp.einsum("het,ts->hes", rates, upper, precision=lax.Precision.HIGHEST)
    middle = total[:, :, span // 2 : span // 2 + 1]
    end = total[:, :, -1:]
    kinds = jnp.stack(
        [
            read[None] * jnp.exp(total - middle),
            read[None] * jnp.exp(total),
            mask[None] * jnp.exp(end - total),
        ],
        1,
    )
    count = memories + 1
    columns = kinds.reshape(groups, held * 3 * count, span).transpose(0, 2, 1)
    columns = jnp.pad(columns, ((0, 0), (0, 0), (0, 128 - held * 3 * count)))
    across = (mask[None] * jnp.exp(middle - total)).reshape(groups, held * count, span)
    decay = jnp.broadcast_to(jnp.exp(end), total.shape).reshape(groups, held * count, span)
    room = ((0, 0), (0, PAD - held * count), (0, 0))
    rows = jnp.concatenate([jnp.pad(across, room), jnp.pad(decay, room)], 1)
    return columns, rows


def kernel(
    groups,
    n_i,
    n_o,
    held,
    count,
    q_ref,
    k_ref,
    v_ref,
    g_ref,
    col_ref,
    row_ref,
    o0_ref,
    o1_ref,
    o2_ref,
    o3_ref,
    x,
    cols,
    rows,
    outs,
    kbs,
    qas,
    local_f,
    local_b,
    run_f,
    run_b,
    enter_f,
    enter_b,
    near_f,
    near_b,
    block_decay,
    derived,
    wire_out,
    wire_in,
    in_send,
    in_recv,
    dec_send,
    dec_recv,
    wire_send,
    wire_recv,
    out_send,
    out_recv,
    own_sem,
):
    span = x.shape[2]
    width = held * DK
    me = lax.axis_index("mem")
    i = lax.axis_index("seqi")
    o = lax.axis_index("seqo")
    inputs = (q_ref, k_ref, v_ref, g_ref)
    outputs = (o0_ref, o1_ref, o2_ref, o3_ref)

    barrier = pltpu.get_barrier_semaphore()
    for off in range(1, groups):
        pl.semaphore_signal(
            barrier, inc=1, device_id={"mem": lax.rem(me + off, groups)}, device_id_type=MESH
        )
    for off in range(1, n_o):
        pl.semaphore_signal(
            barrier, inc=1, device_id={"seqo": lax.rem(o + off, n_o)}, device_id_type=MESH
        )

    @pl.when(i > 0)
    def _():
        pl.semaphore_signal(
            barrier, inc=1, device_id={"seqi": lax.rem(i + n_i - 1, n_i)}, device_id_type=MESH
        )

    @pl.when(i < n_i - 1)
    def _():
        pl.semaphore_signal(
            barrier, inc=1, device_id={"seqi": lax.rem(i + 1, n_i)}, device_id_type=MESH
        )

    sides = jnp.where(i > 0, 1, 0) + jnp.where(i < n_i - 1, 1, 0)
    pl.semaphore_wait(barrier, groups - 1 + n_o - 1 + sides)

    arriving = []
    for off in range(1, groups):
        to = lax.rem(me + off, groups)
        lanes = pl.ds(pl.multiple_of(to * width, width), width)
        pairs = [(ref.at[:, lanes], x.at[a, me]) for a, ref in enumerate(inputs)]
        pairs += [(col_ref.at[to], cols.at[me]), (row_ref.at[to], rows.at[me])]
        for a, (src, dst) in enumerate(pairs):
            copy = pltpu.make_async_remote_copy(
                src_ref=src,
                dst_ref=dst,
                send_sem=in_send.at[off - 1, a],
                recv_sem=in_recv.at[off - 1, a],
                device_id={"mem": to},
                device_id_type=MESH,
            )
            copy.start()
            arriving.append(copy)
    lanes = pl.ds(pl.multiple_of(me * width, width), width)
    pairs = [(ref.at[:, lanes], x.at[a, me]) for a, ref in enumerate(inputs)]
    pairs += [(col_ref.at[me], cols.at[me]), (row_ref.at[me], rows.at[me])]
    own = []
    for a, (src, dst) in enumerate(pairs):
        copy = pltpu.make_async_copy(src, dst, own_sem.at[a])
        copy.start()
        own.append(copy)
    for copy in own:
        copy.wait()
    for copy in arriving:
        copy.wait()

    chunk_decay = [rows[c, PAD:] for c in range(groups)]
    total = jnp.ones((PAD, span), F32)
    for c in range(groups):
        near_f[c] = total
        total = total * chunk_decay[c]
    block_decay[o] = total
    after = jnp.ones((PAD, span), F32)
    for c in reversed(range(groups)):
        near_b[c] = after
        after = after * chunk_decay[c]
    decays = []
    for off in range(1, n_o):
        copy = pltpu.make_async_remote_copy(
            src_ref=block_decay.at[o],
            dst_ref=block_decay.at[o],
            send_sem=dec_send.at[off - 1],
            recv_sem=dec_recv.at[off - 1],
            device_id={"seqo": lax.rem(o + off, n_o)},
            device_id_type=MESH,
        )
        copy.start()
        decays.append(copy)

    run_f[...] = jnp.zeros_like(run_f)
    run_b[...] = jnp.zeros_like(run_b)

    def gather_states(step, carry):
        c = step
        z = groups - 1 - step
        for h in range(held):
            lanes = slice(h * DK, (h + 1) * DK)
            base = h * 3 * count
            col = cols[c]
            key = x[1, c, :, lanes].astype(F32)
            kb = jnp.concatenate(
                [
                    (key * col[:, base + 2 * count + e : base + 2 * count + e + 1]).astype(BF16)
                    for e in range(count)
                ],
                1,
            )
            kbs[c, h] = kb
            state = dot(kb, x[2, c, :, lanes], 0, 0)
            for e in range(count):
                r = slice(e * DK, (e + 1) * DK)
                d = rows[c, PAD + h * count + e : PAD + h * count + e + 1, :]
                old = run_f[h, r, :]
                local_f[c, h, r, :] = old
                run_f[h, r, :] = old * d + state[r]
            col = cols[z]
            query = x[0, z, :, lanes].astype(F32)
            qa = jnp.concatenate(
                [
                    (query * col[:, base + count + e : base + count + e + 1]).astype(BF16)
                    for e in range(count)
                ],
                1,
            )
            qas[z, h] = qa
            state = dot(qa, x[3, z, :, lanes], 0, 0)
            for e in range(count):
                r = slice(e * DK, (e + 1) * DK)
                d = rows[z, PAD + h * count + e : PAD + h * count + e + 1, :]
                old = run_b[h, r, :]
                local_b[z, h, r, :] = old
                run_b[h, r, :] = old * d + state[r]
        return carry

    lax.fori_loop(0, groups, gather_states, 0)

    for copy in decays:
        copy.wait()
    before = jnp.ones((PAD, span), F32)
    later = jnp.ones((PAD, span), F32)
    for b in range(n_o):
        piece = block_decay[b]
        before = before * jnp.where(b < o, piece, 1.0)
        later = later * jnp.where(b > o, piece, 1.0)
    derived[0] = before
    derived[1] = later
    derived[2] = block_decay[o]
    derived[3] = before * later * block_decay[o]

    def scaled(value, kind, h):
        parts = []
        for e in range(count):
            d = derived[kind, h * count + e : h * count + e + 1, :]
            parts.append(value[e * DK : (e + 1) * DK].astype(F32) * d)
        return jnp.concatenate(parts, 0)

    sent = []

    def hop(w, kind, h, axis, to, allowed):
        copy = pltpu.make_async_remote_copy(
            src_ref=wire_out.at[w, kind, h],
            dst_ref=wire_in.at[w, kind, h],
            send_sem=wire_send.at[w, kind, h],
            recv_sem=wire_recv.at[w, kind, h],
            device_id={axis: to},
            device_id_type=MESH,
        )
        pl.when(allowed)(copy.start)
        sent.append((allowed, copy))

    def receive(w, kind, h, present):
        copy = pltpu.make_async_remote_copy(
            src_ref=wire_out.at[w, kind, h],
            dst_ref=wire_in.at[w, kind, h],
            send_sem=wire_send.at[w, kind, h],
            recv_sem=wire_recv.at[w, kind, h],
            device_id={"seqo": lax.rem(o + 1, n_o)},
            device_id_type=MESH,
        )

        @pl.when(present)
        def _():
            copy.wait_recv()

        @pl.when(jnp.logical_not(present))
        def _():
            wire_in[w, kind, h] = jnp.zeros((count * DK, DK), BF16)

    up, down = lax.rem(o + 1, n_o), lax.rem(o + n_o - 1, n_o)
    i_up, i_down = lax.rem(i + 1, n_i), lax.rem(i + n_i - 1, n_i)
    low, high = o > 0, o < n_o - 1
    i_low, i_high = i > 0, i < n_i - 1
    ways = (
        (run_f, low, high, up, down, i_low, i_high, i_up, 0, 1, enter_f),
        (run_b, high, low, down, up, i_high, i_low, i_down, 1, 0, enter_b),
    )

    for h in range(held):
        for w, (run, has_prev, has_next, nxt, prv, _, i_next, _, _, ahead, _) in enumerate(ways):
            receive(w, 0, h, has_prev)
            wire_out[w, 0, h] = (scaled(wire_in[w, 0, h], 2, h) + run[h]).astype(BF16)
            hop(w, 0, h, "seqo", nxt, has_next)
        for w, (run, has_prev, has_next, nxt, prv, _, i_next, _, _, ahead, _) in enumerate(ways):
            receive(w, 1, h, jnp.logical_and(has_next, i_next))
            wire_out[w, 1, h] = (scaled(run[h], ahead, h) + wire_in[w, 1, h].astype(F32)).astype(
                BF16
            )
            hop(w, 1, h, "seqo", prv, jnp.logical_and(has_prev, i_next))
    for h in range(held):
        for w, (run, _, _, _, _, i_prev, i_next, i_nxt, behind, ahead, enter) in enumerate(ways):
            receive(w, 2, h, i_prev)
            group = scaled(scaled(wire_in[w, 0, h], 2, h), ahead, h) + wire_out[w, 1, h].astype(F32)
            wire_out[w, 2, h] = (scaled(wire_in[w, 2, h], 3, h) + group).astype(BF16)
            hop(w, 2, h, "seqi", i_nxt, i_next)
            enter[h] = scaled(wire_in[w, 2, h], behind, h) + wire_in[w, 0, h].astype(F32)

    lower = lax.broadcasted_iota(jnp.int32, (span, span), 0) >= lax.broadcasted_iota(
        jnp.int32, (span, span), 1
    )

    def leaving(step, a):
        to = lax.rem(me + 1 + step, groups)
        lanes = pl.ds(pl.multiple_of(me * width, width), width)
        return pltpu.make_async_remote_copy(
            src_ref=outs.at[a, to],
            dst_ref=outputs[a].at[:, lanes],
            send_sem=out_send.at[step, a],
            recv_sem=out_recv.at[step, a],
            device_id={"mem": to},
            device_id_type=MESH,
        )

    def finish(step, carry):
        c = lax.rem(me + 1 + step, groups)
        col = cols[c]
        for h in range(held):
            lanes = slice(h * DK, (h + 1) * DK)
            base = h * 3 * count
            q, k, v, g = (x[a, c, :, lanes] for a in range(4))
            weight = jnp.zeros((span, span), F32)
            for e in range(count):
                j = h * count + e
                weight += col[:, base + e : base + e + 1] * rows[c, j : j + 1, :]
            weight = jnp.where(lower, weight, 0.0)
            sw = (dot(q, k, 1, 1) * weight).astype(BF16)
            gw = (dot(g, v, 1, 1) * weight).astype(BF16)
            past, future = [], []
            for e in range(count):
                j = h * count + e
                r = slice(e * DK, (e + 1) * DK)
                past.append(
                    (local_f[c, h, r, :] + enter_f[h, r, :] * near_f[c, j : j + 1, :]).astype(BF16)
                )
                future.append(
                    (local_b[c, h, r, :] + enter_b[h, r, :] * near_b[c, j : j + 1, :]).astype(BF16)
                )
            past = jnp.concatenate(past, 0)
            future = jnp.concatenate(future, 0)
            out = dot(sw, v, 1, 0) + dot(qas[c, h], past, 1, 0)
            grad_v = dot(sw, g, 0, 0) + dot(kbs[c, h], future, 1, 0)
            grad_q = dot(gw, k, 1, 0)
            grad_k = dot(gw, q, 0, 0)
            from_past = dot(g, past, 1, 1)
            from_future = dot(v, future, 1, 1)
            for e in range(count):
                r = slice(e * DK, (e + 1) * DK)
                ra = base + count + e
                rb = base + 2 * count + e
                grad_q += from_past[:, r] * col[:, ra : ra + 1]
                grad_k += from_future[:, r] * col[:, rb : rb + 1]
            for a, value in enumerate((out, grad_q, grad_k, grad_v)):
                outs[a, c, :, lanes] = value.astype(BF16)

        @pl.when(step < groups - 1)
        def _():
            for a in range(4):
                leaving(step, a).start()

        return carry

    lax.fori_loop(0, groups, finish, 0)
    lanes = pl.ds(pl.multiple_of(me * width, width), width)
    own = []
    for a in range(4):
        copy = pltpu.make_async_copy(outs.at[a, me], outputs[a].at[:, lanes], own_sem.at[a])
        copy.start()
        own.append(copy)
    for copy in own:
        copy.wait()
    for allowed, copy in sent:
        pl.when(allowed)(copy.wait_send)
    for step in range(groups - 1):
        for a in range(4):
            leaving(step, a).wait()


def body(queries, keys, values, log_decay, routes, route_logits, cotangent):
    groups = lax.axis_size("mem")
    n_i = lax.axis_size("seqi")
    n_o = lax.axis_size("seqo")
    memories = MEM_DEV * groups
    span, features = queries.shape[1:]
    heads = log_decay.shape[0]
    held = heads // groups
    count = memories + 1
    scale = 2.0 / math.sqrt(DK * span * groups * n_i * n_o)
    columns, rows = tables(
        log_decay[:, 0, :].astype(F32),
        routes[0],
        route_logits[0].astype(F32),
        groups,
        memories,
        scale,
    )
    any_spec = pl.BlockSpec(memory_space=pl.ANY)
    state = (held, count * DK, DK)
    result = jax.ShapeDtypeStruct((span, features), BF16)
    dma = pltpu.SemaphoreType.DMA
    results = pl.pallas_call(
        functools.partial(kernel, groups, n_i, n_o, held, count),
        out_shape=[result] * 4,
        in_specs=[any_spec] * 6,
        out_specs=[any_spec] * 4,
        scratch_shapes=[
            pltpu.VMEM((4, groups, span, held * DK), BF16),
            pltpu.VMEM((groups, span, 128), F32),
            pltpu.VMEM((groups, 2 * PAD, span), F32),
            pltpu.VMEM((4, groups, span, held * DK), BF16),
            pltpu.VMEM((groups, held, span, count * DK), BF16),
            pltpu.VMEM((groups, held, span, count * DK), BF16),
            pltpu.VMEM((groups,) + state, F32),
            pltpu.VMEM((groups,) + state, F32),
            pltpu.VMEM(state, F32),
            pltpu.VMEM(state, F32),
            pltpu.VMEM(state, F32),
            pltpu.VMEM(state, F32),
            pltpu.VMEM((groups, PAD, span), F32),
            pltpu.VMEM((groups, PAD, span), F32),
            pltpu.VMEM((n_o, PAD, span), F32),
            pltpu.VMEM((4, PAD, span), F32),
            pltpu.VMEM((2, 3) + state, BF16),
            pltpu.VMEM((2, 3) + state, BF16),
            dma((groups - 1, 6)),
            dma((groups - 1, 6)),
            dma((n_o - 1,)),
            dma((n_o - 1,)),
            dma((2, 3, held)),
            dma((2, 3, held)),
            dma((groups - 1, 4)),
            dma((groups - 1, 4)),
            dma((6,)),
        ],
        compiler_params=pltpu.CompilerParams(
            collective_id=0, has_side_effects=True, vmem_limit_bytes=56 * 1024 * 1024
        ),
        cost_estimate=pl.CostEstimate(
            flops=2 * 36 * heads * DK * DK * span,
            bytes_accessed=16 * span * features,
            transcendentals=0,
        ),
    )(queries[0], keys[0], values[0], cotangent[0], columns, rows)
    return tuple(item[None] for item in results)


def solution(mesh):
    rows = P(("seqi", "seqo"), "mem", None)
    return jax.shard_map(
        body,
        mesh=mesh,
        in_specs=(rows, rows, rows, P(None, ("seqi", "seqo"), "mem"), rows, rows, rows),
        out_specs=(rows, rows, rows, rows),
        check_vma=False,
    )
```

time: 561 us -> 201 us (0.36); the launches traced: 552 us -> 201 us
  Pallas kernels: 0 us -> 190 us
  local copies, waits for them, and re-layouts: 181 us -> 8.78 us
  other arithmetic: 123 us -> 0.81 us
  matrix products: 103 us -> 0.17 us
  waiting for transfers between devices: 62.8 us -> 0 us
  starting transfers between devices: 45.8 us -> 0 us
  blocking collectives: 18.6 us -> 0 us
  between operations: 16.3 us -> 0.75 us
    pallas_call x0 -> x1, Pallas kernels: none -> 190 us  [body(): pl.pallas_call(functools.partial(kernel, groups, n_i, n_o, held, count),...]
    dot_general x36 -> x1, matrix products: 103 us -> 0.17 us  [tables(): jnp.einsum('het,ts->hes', rates, upper, precision=lax.Precision.HIGHEST)]
    all_to_all x11 -> x0, waiting for transfers between devices: 61.2 us -> none  [the longest x1 23.9 us: body(): lax.all_to_all(packed, 'mem', split_axis=0, concat_axis=0, tiled=True)]
    all_to_all x11 -> x0, starting transfers between devices: 45.2 us -> none  [the longest x1 5.16 us: body(): lax.all_to_all(weight_rows, 'mem', split_axis=0, concat_axis=0, tiled=True)]
    gather x5 -> x0, local copies, waits for them, and re-layouts: 32.5 us -> none  [the longest x1 13.2 us: body(): packed = stacked[slot_table].reshape(groups, MEM_DEV, CAP, 3, features)]
    select_n x17 -> x0, other arithmetic: 32 us -> none  [the longest x14 32 us: hop(): jnp.where(position < mine, new, old)]
    another operation x27 -> x1, local copies, waits for them, and re-layouts: 30.3 us -> 0.05 us  [tables(): jnp.stack([read[None] * jnp.exp(total - middle), read[None] * jnp.exp(tot...]
    add x18 -> x1, other arithmetic: 28.8 us -> 0.01 us  [tables(): first[None] * hit_first + second[None] * hit_second]
  transfers between devices with their start and end apart: 13 -> 0, of which waited for: 9 -> 0; matrix products, arithmetic and copies ran while one was open for 59% -> 0% of each run, Pallas kernels for 0% -> 0%
where the time goes in v1:
time: 201 us
  Pallas kernels  190 us (95%)
  local copies, waits for them, and re-layouts  8.78 us (4%)
    pallas_call x1, Pallas kernels, body(): pl.pallas_call(functools.partial(kernel, groups, n_i, n_o, held, count),...  190 us
    unnamed x17, local copies, waits for them, and re-layouts  7.3 us

profile of v1, /device:TPU:0, one launch (start us, length us, event | category | flops | bytes accessed | tf_op | source)
XLA Modules:
  0.0 200.8 jit_solution(2836218052026886349)
XLA Ops:
  0.6 0.0 copy-start.5
  0.6 0.6 copy-done.5
  1.3 0.0 copy-start.4
  1.3 0.7 copy-done.4
  2.0 0.0 copy-start.3
  2.0 0.7 copy-done.3
  2.7 0.2 fusion.1
  2.9 0.2 slice_exponential_fusion
  3.0 0.2 copy.21
  3.2 0.1 broadcast_in_dim.12
  3.3 0.1 copy.22
  3.4 0.1 broadcast_in_dim.13
  3.5 0.1 exponential_multiply_fusion
  3.7 0.6 select_maximum_fusion.row_ref
  4.3 0.1 copy.18
  4.4 0.1 copy.19
  4.6 0.7 pad.13.col_ref
  5.3 190.3 %shard_map.102 = (bf16[128,2048]{1,0:T(8,128)(2,1)}, bf16[128,2048]{1,0:T(8,128)(2,1)}, bf16[128,2048]{1,0:T(8,128)(2,1)}, bf16[128,2048]{1,0:T(8,128)(2,1)}) custom-call(bf16[128,2048]{1,0:T(8,128)(2,1)} %bitcast.45, bf16[128,2048]{1,0:T(8,128)(2,1)} %bitcast.46, bf16[128,2048]{1,0:T(8,128)(2,1)} %bitcast.47, bf16[128,2048]{1,0:T(8,128)(2,1)} %bitcast.48, ...), custom_call_target="tpu_custom_call" | custom-call | flops 2415919104 | bytes 4194304 | tf_op jit(solution)/shard_map/pallas_call | solution.py:418
  195.6 0.0 copy-start.2
  195.6 1.9 copy.31
  197.5 0.0 copy-done.2
  197.5 0.0 copy-start.1
  197.6 0.8 copy.32
  198.3 0.4 copy-done.1
  198.8 0.0 copy-start
  198.8 0.8 copy.33
  199.6 0.4 copy-done
  200.0 0.8 copy.34
  (11 shorter events, 0.1 us)
Async XLA Ops:
  0.6 0.7 copy-start.5
  1.3 0.7 copy-start.4
  2.0 0.7 copy-start.3
  195.6 2.0 copy-start.2
  197.5 1.2 copy-start.1
  198.8 1.2 copy-start

commit v2 on v1

v2 whole, which is shorter than its diff:
```python
import functools
import math

import jax
import jax.numpy as jnp
from jax import lax
from jax.experimental import pallas as pl
from jax.experimental.pallas import tpu as pltpu
from jax.sharding import PartitionSpec as P

DK = 128
MEM_DEV = 1
MESH = pl.DeviceIdType.MESH
F32 = jnp.float32
BF16 = jnp.bfloat16


def dot(left, right, left_dim, right_dim):
    return lax.dot_general(
        left, right, (((left_dim,), (right_dim,)), ((), ())), preferred_element_type=F32
    )


def tables(gates, chosen, logits, groups, memories, scale):
    heads, span = gates.shape
    held = heads // groups
    first = jax.nn.sigmoid(logits[:, 0] - logits[:, 1]).astype(BF16).astype(F32)
    second = jax.nn.sigmoid(logits[:, 1] - logits[:, 0]).astype(BF16).astype(F32)
    names = jnp.arange(memories, dtype=jnp.int32)[:, None]
    hit_first = (chosen[:, 0][None, :] == names).astype(F32)
    hit_second = (chosen[:, 1][None, :] == names).astype(F32)
    ones = jnp.ones((1, span), F32)
    mask = jnp.concatenate([hit_first + hit_second, ones], 0)
    read = jnp.concatenate([first[None] * hit_first + second[None] * hit_second, ones], 0) * scale
    rates = gates[:, None, :] * mask[None]
    upper = (jnp.arange(span)[:, None] <= jnp.arange(span)[None, :]).astype(F32)
    total = jnp.einsum("het,ts->hes", rates, upper, precision=lax.Precision.HIGHEST)
    middle = total[:, :, span // 2 : span // 2 + 1]
    end = total[:, :, -1:]
    count = memories + 1
    kinds = jnp.concatenate(
        [
            read[None] * jnp.exp(total - middle),
            read[None] * jnp.exp(total),
            mask[None] * jnp.exp(end - total),
            jnp.zeros((heads, 16 - 3 * count, span), F32),
            mask[None] * jnp.exp(middle - total),
            jnp.zeros((heads, 8 - count, span), F32),
            jnp.broadcast_to(jnp.exp(end), total.shape),
            jnp.zeros((heads, 8 - count, span), F32),
        ],
        1,
    )
    return kinds.reshape(groups, held, 32, span)


def kernel(
    groups,
    n_i,
    n_o,
    held,
    count,
    q_ref,
    k_ref,
    v_ref,
    g_ref,
    row_ref,
    o0_ref,
    o1_ref,
    o2_ref,
    o3_ref,
    x,
    rows,
    cols,
    outs,
    part,
    kbs,
    qas,
    local_f,
    local_b,
    run_f,
    run_b,
    enter_f,
    enter_b,
    near_f,
    near_b,
    block_decay,
    derived,
    wire_out,
    wire_in,
    row_send,
    row_recv,
    in_send,
    in_recv,
    dec_send,
    dec_recv,
    wire_send,
    wire_recv,
    out_send,
    out_recv,
    row_sem,
    own_sem,
):
    span = x.shape[3]
    width = held * DK
    me = lax.axis_index("mem")
    i = lax.axis_index("seqi")
    o = lax.axis_index("seqo")
    inputs = (q_ref, k_ref, v_ref, g_ref)
    outputs = (o0_ref, o1_ref, o2_ref, o3_ref)

    barrier = pltpu.get_barrier_semaphore()
    for off in range(1, groups):
        pl.semaphore_signal(
            barrier, inc=1, device_id={"mem": lax.rem(me + off, groups)}, device_id_type=MESH
        )
    for off in range(1, n_o):
        pl.semaphore_signal(
            barrier, inc=1, device_id={"seqo": lax.rem(o + off, n_o)}, device_id_type=MESH
        )

    @pl.when(i > 0)
    def _():
        pl.semaphore_signal(
            barrier, inc=1, device_id={"seqi": lax.rem(i + n_i - 1, n_i)}, device_id_type=MESH
        )

    @pl.when(i < n_i - 1)
    def _():
        pl.semaphore_signal(
            barrier, inc=1, device_id={"seqi": lax.rem(i + 1, n_i)}, device_id_type=MESH
        )

    sides = jnp.where(i > 0, 1, 0) + jnp.where(i < n_i - 1, 1, 0)
    pl.semaphore_wait(barrier, groups - 1 + n_o - 1 + sides)

    def row_copy(off):
        to = lax.rem(me + off, groups)
        return pltpu.make_async_remote_copy(
            src_ref=row_ref.at[to],
            dst_ref=rows.at[me],
            send_sem=row_send.at[off - 1],
            recv_sem=row_recv.at[off - 1],
            device_id={"mem": to},
            device_id_type=MESH,
        )

    def in_copy(off, h, a):
        to = lax.rem(me + off, groups)
        lanes = pl.ds(pl.multiple_of((to * held + h) * DK, DK), DK)
        return pltpu.make_async_remote_copy(
            src_ref=inputs[a].at[:, lanes],
            dst_ref=x.at[a, h, me],
            send_sem=in_send.at[off - 1, h, a],
            recv_sem=in_recv.at[off - 1, h, a],
            device_id={"mem": to},
            device_id_type=MESH,
        )

    def own_copy(h, a):
        lanes = pl.ds(pl.multiple_of((me * held + h) * DK, DK), DK)
        return pltpu.make_async_copy(inputs[a].at[:, lanes], x.at[a, h, me], own_sem.at[h, a])

    for off in range(1, groups):
        row_copy(off).start()
    own_rows = pltpu.make_async_copy(row_ref.at[me], rows.at[me], row_sem)
    own_rows.start()

    def start_in(h, carry):
        for a in range(4):
            for off in range(1, groups):
                in_copy(off, h, a).start()
            own_copy(h, a).start()
        return carry

    lax.fori_loop(0, held, start_in, 0)
    own_rows.wait()
    for off in range(1, groups):
        row_copy(off).wait()

    chunk_decay = [rows[c, :, 24:32, :] for c in range(groups)]
    total = jnp.ones((held, 8, span), F32)
    for c in range(groups):
        near_f[c] = total
        total = total * chunk_decay[c]
    block_decay[o] = total
    after = jnp.ones((held, 8, span), F32)
    for c in reversed(range(groups)):
        near_b[c] = after
        after = after * chunk_decay[c]
    decays = []
    for off in range(1, n_o):
        copy = pltpu.make_async_remote_copy(
            src_ref=block_decay.at[o],
            dst_ref=block_decay.at[o],
            send_sem=dec_send.at[off - 1],
            recv_sem=dec_recv.at[off - 1],
            device_id={"seqo": lax.rem(o + off, n_o)},
            device_id_type=MESH,
        )
        copy.start()
        decays.append(copy)

    def block(e):
        return slice(e * DK, (e + 1) * DK)

    def gather_states(h):
        run_f[h] = jnp.zeros((DK, count * DK), F32)
        run_b[h] = jnp.zeros((DK, count * DK), F32)
        for c in range(groups):
            col = rows[c, h, 0:16, :].T
            cols[c, h] = col
            for a, saved, first in ((1, kbs, 2 * count), (0, qas, count)):
                value = x[a, h, c].astype(F32)
                saved[c, h] = jnp.concatenate(
                    [
                        (value * col[:, first + e : first + e + 1]).astype(BF16)
                        for e in range(count)
                    ],
                    1,
                )
        for step in range(groups):
            for c, a, saved, run, local in (
                (step, 2, kbs, run_f, local_f),
                (groups - 1 - step, 3, qas, run_b, local_b),
            ):
                state = dot(x[a, h, c], saved[c, h], 0, 0)
                for e in range(count):
                    old = run[h, :, block(e)]
                    local[c, h, :, block(e)] = old
                    run[h, :, block(e)] = old * rows[c, h, 24 + e : 25 + e, :] + state[:, block(e)]

    lower = lax.broadcasted_iota(jnp.int32, (span, span), 0) >= lax.broadcasted_iota(
        jnp.int32, (span, span), 1
    )

    def within(h):
        for c in range(groups):
            q, k, v, g = (x[a, h, c] for a in range(4))
            col = cols[c, h]
            weight = jnp.zeros((span, span), F32)
            for e in range(count):
                weight += col[:, e : e + 1] * rows[c, h, 16 + e : 17 + e, :]
            weight = jnp.where(lower, weight, 0.0)
            sw = (dot(q, k, 1, 1) * weight).astype(BF16)
            gw = (dot(g, v, 1, 1) * weight).astype(BF16)
            part[0, c, h] = dot(sw, v, 1, 0)
            part[1, c, h] = dot(gw, k, 1, 0)
            part[2, c, h] = dot(gw, q, 0, 0)
            part[3, c, h] = dot(sw, g, 0, 0)

    def scaled(value, kind, h):
        return jnp.concatenate(
            [
                value[:, block(e)].astype(F32) * derived[kind, h, e : e + 1, :]
                for e in range(count)
            ],
            1,
        )

    def hop(w, kind, h, axis, to):
        return pltpu.make_async_remote_copy(
            src_ref=wire_out.at[w, kind, h],
            dst_ref=wire_in.at[w, kind, h],
            send_sem=wire_send.at[w, kind, h],
            recv_sem=wire_recv.at[w, kind, h],
            device_id={axis: to},
            device_id_type=MESH,
        )

    up, down = lax.rem(o + 1, n_o), lax.rem(o + n_o - 1, n_o)
    i_up, i_down = lax.rem(i + 1, n_i), lax.rem(i + n_i - 1, n_i)
    low, high = o > 0, o < n_o - 1
    i_low, i_high = i > 0, i < n_i - 1
    runs = (run_f, run_b)
    enters = (enter_f, enter_b)
    along = ((low, high, up), (high, low, down))
    across = ((i_low, i_high, i_up), (i_high, i_low, i_down))
    links = []
    for w in range(2):
        links.append((w, 0, "seqo") + along[w])
        has, to_has, to = along[1 - w]
        passes = across[w][1]
        links.append(
            (w, 1, "seqo", jnp.logical_and(has, passes), jnp.logical_and(to_has, passes), to)
        )
        links.append((w, 2, "seqi") + across[w])
    links = {(w, kind): rest for w, kind, *rest in links}

    def receive(w, kind, h):
        axis, present, _, to = links[w, kind]

        @pl.when(present)
        def _():
            hop(w, kind, h, axis, to).wait_recv()

        @pl.when(jnp.logical_not(present))
        def _():
            wire_in[w, kind, h] = jnp.zeros((DK, count * DK), BF16)

    def send(w, kind, h):
        axis, _, allowed, to = links[w, kind]

        @pl.when(allowed)
        def _():
            hop(w, kind, h, axis, to).start()

    def prefix(w, h):
        receive(w, 0, h)
        wire_out[w, 0, h] = (scaled(wire_in[w, 0, h], 2, h) + runs[w][h]).astype(BF16)
        send(w, 0, h)

    def rest(w, h):
        receive(w, 1, h)
        wire_out[w, 1, h] = (
            scaled(runs[w][h], 1 - w, h) + wire_in[w, 1, h].astype(F32)
        ).astype(BF16)
        send(w, 1, h)

    def slot(t, carry):
        @pl.when(t < held)
        def _():
            for a in range(4):
                own_copy(t, a).wait()
                for off in range(1, groups):
                    in_copy(off, t, a).wait_recv()
            gather_states(t)

        @pl.when(t == 0)
        def _():
            for copy in decays:
                copy.wait()
            before = jnp.ones((held, 8, span), F32)
            later = jnp.ones((held, 8, span), F32)
            for b in range(n_o):
                piece = block_decay[b]
                before = before * jnp.where(b < o, piece, 1.0)
                later = later * jnp.where(b > o, piece, 1.0)
            derived[0] = before
            derived[1] = later
            derived[2] = block_decay[o]
            derived[3] = before * later * block_decay[o]

        rising = t - o
        falling = t - (n_o - 1 - o)

        @pl.when(jnp.logical_and(rising >= 0, rising < held))
        def _():
            prefix(0, rising)
            rest(1, rising)

        @pl.when(jnp.logical_and(falling >= 0, falling < held))
        def _():
            prefix(1, falling)
            rest(0, falling)

        @pl.when(t >= n_o - 1)
        def _():
            within(t - (n_o - 1))

        return carry

    lax.fori_loop(0, held + n_o - 1, slot, 0)

    def entering(w):
        def one(h, carry):
            group = scaled(scaled(wire_in[w, 0, h], 2, h), 1 - w, h)
            group += wire_out[w, 1, h].astype(F32)
            receive(w, 2, h)
            wire_out[w, 2, h] = (scaled(wire_in[w, 2, h], 3, h) + group).astype(BF16)
            send(w, 2, h)
            enters[w][h] = scaled(wire_in[w, 2, h], w, h) + wire_in[w, 0, h].astype(F32)
            return carry

        lax.fori_loop(0, held, one, 0)

    early = 2 * i < n_i

    @pl.when(early)
    def _():
        entering(0)
        entering(1)

    @pl.when(jnp.logical_not(early))
    def _():
        entering(1)
        entering(0)

    def leaving(step, a):
        to = lax.rem(me + 1 + step, groups)
        lanes = pl.ds(pl.multiple_of(me * width, width), width)
        return pltpu.make_async_remote_copy(
            src_ref=outs.at[a, to],
            dst_ref=outputs[a].at[:, lanes],
            send_sem=out_send.at[step, a],
            recv_sem=out_recv.at[step, a],
            device_id={"mem": to},
            device_id_type=MESH,
        )

    def finish(step, carry):
        c = lax.rem(me + 1 + step, groups)
        for h in range(held):
            col = cols[c, h]
            past, future = (
                jnp.concatenate(
                    [
                        (
                            local[c, h, :, block(e)]
                            + enter[h, :, block(e)] * near[c, h, e : e + 1, :]
                        ).astype(BF16)
                        for e in range(count)
                    ],
                    1,
                )
                for local, enter, near in (
                    (local_f, enter_f, near_f),
                    (local_b, enter_b, near_b),
                )
            )
            out = part[0, c, h] + dot(qas[c, h], past, 1, 1)
            grad_v = part[3, c, h] + dot(kbs[c, h], future, 1, 1)
            grad_q = part[1, c, h]
            grad_k = part[2, c, h]
            from_past = dot(x[3, h, c], past, 1, 0)
            from_future = dot(x[2, h, c], future, 1, 0)
            for e in range(count):
                grad_q += from_past[:, block(e)] * col[:, count + e : count + e + 1]
                grad_k += from_future[:, block(e)] * col[:, 2 * count + e : 2 * count + e + 1]
            for a, value in enumerate((out, grad_q, grad_k, grad_v)):
                outs[a, c, :, block(h)] = value.astype(BF16)

        @pl.when(step < groups - 1)
        def _():
            for a in range(4):
                leaving(step, a).start()

        return carry

    lax.fori_loop(0, groups, finish, 0)
    lanes = pl.ds(pl.multiple_of(me * width, width), width)
    own = []
    for a in range(4):
        copy = pltpu.make_async_copy(outs.at[a, me], outputs[a].at[:, lanes], own_sem.at[0, a])
        copy.start()
        own.append(copy)
    for copy in own:
        copy.wait()

    def drain(h, carry):
        for a in range(4):
            for off in range(1, groups):
                in_copy(off, h, a).wait_send()
        for (w, kind), (axis, _, allowed, to) in links.items():

            @pl.when(allowed)
            def _():
                hop(w, kind, h, axis, to).wait_send()

        return carry

    lax.fori_loop(0, held, drain, 0)
    for step in range(groups - 1):
        for a in range(4):
            leaving(step, a).wait()


def body(queries, keys, values, log_decay, routes, route_logits, cotangent):
    groups = lax.axis_size("mem")
    n_i = lax.axis_size("seqi")
    n_o = lax.axis_size("seqo")
    memories = MEM_DEV * groups
    span, features = queries.shape[1:]
    heads = log_decay.shape[0]
    held = heads // groups
    count = memories + 1
    scale = 2.0 / math.sqrt(DK * span * groups * n_i * n_o)
    rows = tables(
        log_decay[:, 0, :].astype(F32),
        routes[0],
        route_logits[0].astype(F32),
        groups,
        memories,
        scale,
    )
    any_spec = pl.BlockSpec(memory_space=pl.ANY)
    state = (held, DK, count * DK)
    result = jax.ShapeDtypeStruct((span, features), BF16)
    dma = pltpu.SemaphoreType.DMA
    results = pl.pallas_call(
        functools.partial(kernel, groups, n_i, n_o, held, count),
        out_shape=[result] * 4,
        in_specs=[any_spec] * 5,
        out_specs=[any_spec] * 4,
        scratch_shapes=[
            pltpu.VMEM((4, held, groups, span, DK), BF16),
            pltpu.VMEM((groups, held, 32, span), F32),
            pltpu.VMEM((groups, held, span, 16), F32),
            pltpu.VMEM((4, groups, span, held * DK), BF16),
            pltpu.VMEM((4, groups, held, span, DK), F32),
            pltpu.VMEM((groups, held, span, count * DK), BF16),
            pltpu.VMEM((groups, held, span, count * DK), BF16),
            pltpu.VMEM((groups,) + state, F32),
            pltpu.VMEM((groups,) + state, F32),
            pltpu.VMEM(state, F32),
            pltpu.VMEM(state, F32),
            pltpu.VMEM(state, F32),
            pltpu.VMEM(state, F32),
            pltpu.VMEM((groups, held, 8, span), F32),
            pltpu.VMEM((groups, held, 8, span), F32),
            pltpu.VMEM((n_o, held, 8, span), F32),
            pltpu.VMEM((4, held, 8, span), F32),
            pltpu.VMEM((2, 3) + state, BF16),
            pltpu.VMEM((2, 3) + state, BF16),
            dma((groups - 1,)),
            dma((groups - 1,)),
            dma((groups - 1, held, 4)),
            dma((groups - 1, held, 4)),
            dma((n_o - 1,)),
            dma((n_o - 1,)),
            dma((2, 3, held)),
            dma((2, 3, held)),
            dma((groups - 1, 4)),
            dma((groups - 1, 4)),
            dma,
            dma((held, 4)),
        ],
        compiler_params=pltpu.CompilerParams(
            collective_id=0, has_side_effects=True, vmem_limit_bytes=56 * 1024 * 1024
        ),
        cost_estimate=pl.CostEstimate(
            flops=2 * 36 * heads * DK * DK * span,
            bytes_accessed=16 * span * features,
            transcendentals=0,
        ),
    )(queries[0], keys[0], values[0], cotangent[0], rows)
    return tuple(item[None] for item in results)


def solution(mesh):
    rows = P(("seqi", "seqo"), "mem", None)
    return jax.shard_map(
        body,
        mesh=mesh,
        in_specs=(rows, rows, rows, P(None, ("seqi", "seqo"), "mem"), rows, rows, rows),
        out_specs=(rows, rows, rows, rows),
        check_vma=False,
    )
```

time: 201 us -> 92.7 us (0.46)
  Pallas kernels: 190 us -> 82.9 us
    pallas_call x1, Pallas kernels: 190 us -> 82.9 us  [body(): pl.pallas_call(functools.partial(kernel, groups, n_i, n_o, held, count),...]
    unnamed x17 -> x19, local copies, waits for them, and re-layouts: 7.3 us -> 7.27 us
where the time goes in v2:
time: 92.7 us; the launch traced here: 92.4 us
  Pallas kernels  82.9 us (89%)
  local copies, waits for them, and re-layouts  8.25 us (9%)
    pallas_call x1, Pallas kernels, body(): pl.pallas_call(functools.partial(kernel, groups, n_i, n_o, held, count),...  82.9 us
    unnamed x19, local copies, waits for them, and re-layouts  7.27 us

profile of v2, /device:TPU:0, one launch (start us, length us, event | category | flops | bytes accessed | tf_op | source)
XLA Modules:
  0.0 92.4 jit_solution(1042316266300214460)
XLA Ops:
  0.6 0.0 copy-start.5
  0.6 0.6 copy-done.5
  1.3 0.0 copy-start.4
  1.3 0.7 copy-done.4
  2.0 0.0 copy-start.3
  2.0 0.7 copy-done.3
  2.7 0.2 fusion.1
  2.9 0.2 exponential_reduce_fusion
  3.1 0.1 multiply_dynamic-update-slice_fusion.3
  3.2 0.1 multiply_dynamic-update-slice_fusion.1
  3.3 0.1 multiply_dynamic-update-slice_fusion
  3.4 0.1 broadcast_dynamic-update-slice_fusion
  3.5 0.8 copy.12
  4.3 82.9 %shard_map.102 = (bf16[128,2048]{1,0:T(8,128)(2,1)}, bf16[128,2048]{1,0:T(8,128)(2,1)}, bf16[128,2048]{1,0:T(8,128)(2,1)}, bf16[128,2048]{1,0:T(8,128)(2,1)}) custom-call(bf16[128,2048]{1,0:T(8,128)(2,1)} %bitcast.35, bf16[128,2048]{1,0:T(8,128)(2,1)} %bitcast.36, bf16[128,2048]{1,0:T(8,128)(2,1)} %bitcast.37, bf16[128,2048]{1,0:T(8,128)(2,1)} %bitcast.38, ...), custom_call_target="tpu_custom_call" | custom-call | flops 2415919104 | bytes 4194304 | tf_op jit(solution)/shard_map/pallas_call | solution.py:490
  87.2 0.0 copy-start.2
  87.2 1.9 %copy.24 = bf16[1,128,2048]{2,1,0:T(8,128)(2,1)} copy(bf16[1,128,2048]{2,1,0:T(8,128)(2,1)} %bitcast.32) | data formatting | bytes 1048576
  89.1 0.0 copy-done.2
  89.1 0.0 copy-start.1
  89.1 0.8 copy.25
  89.9 0.4 copy-done.1
  90.4 0.0 copy-start
  90.4 0.8 copy.26
  91.2 0.4 copy-done
  91.6 0.8 copy.27
  (11 shorter events, 0.1 us)
Async XLA Ops:
  0.6 0.7 copy-start.5
  1.3 0.7 copy-start.4
  2.0 0.7 copy-start.3
  87.2 2.0 %copy-start.2 = (bf16[128,2048]{1,0:T(8,128)(2,1)S(1)}, bf16[128,2048]{1,0:T(8,128)(2,1)}, u32[]{:S(2)}) copy-start(bf16[128,2048]{1,0:T(8,128)(2,1)} %get-tuple-element.9) | copy-start | bytes 1572868
  89.1 1.2 %copy-start.1 = (bf16[128,2048]{1,0:T(8,128)(2,1)S(1)}, bf16[128,2048]{1,0:T(8,128)(2,1)}, u32[]{:S(2)}) copy-start(bf16[128,2048]{1,0:T(8,128)(2,1)} %get-tuple-element.10) | copy-start | bytes 1572868
  90.4 1.2 %copy-start = (bf16[128,2048]{1,0:T(8,128)(2,1)S(1)}, bf16[128,2048]{1,0:T(8,128)(2,1)}, u32[]{:S(2)}) copy-start(bf16[128,2048]{1,0:T(8,128)(2,1)} %get-tuple-element.11) | copy-start | bytes 1572868

commit v3 on v2

--- a/solution.py
+++ b/solution.py
@@ -65,10 +65,7 @@
     v_ref,
     g_ref,
     row_ref,
-    o0_ref,
-    o1_ref,
-    o2_ref,
-    o3_ref,
+    out_ref,
     x,
     rows,
     cols,
@@ -100,14 +97,13 @@
     out_recv,
     row_sem,
     own_sem,
+    stay_sem,
 ):
     span = x.shape[3]
-    width = held * DK
     me = lax.axis_index("mem")
     i = lax.axis_index("seqi")
     o = lax.axis_index("seqo")
     inputs = (q_ref, k_ref, v_ref, g_ref)
-    outputs = (o0_ref, o1_ref, o2_ref, o3_ref)
 
     barrier = pltpu.get_barrier_semaphore()
     for off in range(1, groups):
@@ -354,53 +350,52 @@
             prefix(1, falling)
             rest(0, falling)
 
-        @pl.when(t >= n_o - 1)
-        def _():
-            within(t - (n_o - 1))
+        @pl.when(t < held)
+        def _():
+            within(t)
+
+        for w, place in ((0, i), (1, n_i - 1 - i)):
+            crossing = t - (n_o - 1) - place
+
+            @pl.when(jnp.logical_and(crossing >= 0, crossing < held))
+            def _():
+                entering(w, crossing)
+
+        done = t - (n_o - 1) - (n_i - 1)
+
+        @pl.when(done >= 0)
+        def _():
+            finish(done)
 
         return carry
 
-    lax.fori_loop(0, held + n_o - 1, slot, 0)
-
-    def entering(w):
-        def one(h, carry):
-            group = scaled(scaled(wire_in[w, 0, h], 2, h), 1 - w, h)
-            group += wire_out[w, 1, h].astype(F32)
-            receive(w, 2, h)
-            wire_out[w, 2, h] = (scaled(wire_in[w, 2, h], 3, h) + group).astype(BF16)
-            send(w, 2, h)
-            enters[w][h] = scaled(wire_in[w, 2, h], w, h) + wire_in[w, 0, h].astype(F32)
-            return carry
-
-        lax.fori_loop(0, held, one, 0)
-
-    early = 2 * i < n_i
-
-    @pl.when(early)
-    def _():
-        entering(0)
-        entering(1)
-
-    @pl.when(jnp.logical_not(early))
-    def _():
-        entering(1)
-        entering(0)
-
-    def leaving(step, a):
+    def entering(w, h):
+        group = scaled(scaled(wire_in[w, 0, h], 2, h), 1 - w, h)
+        group += wire_out[w, 1, h].astype(F32)
+        receive(w, 2, h)
+        wire_out[w, 2, h] = (scaled(wire_in[w, 2, h], 3, h) + group).astype(BF16)
+        send(w, 2, h)
+        enters[w][h] = scaled(wire_in[w, 2, h], w, h) + wire_in[w, 0, h].astype(F32)
+
+    def leaving(step, h, a):
         to = lax.rem(me + 1 + step, groups)
-        lanes = pl.ds(pl.multiple_of(me * width, width), width)
+        lanes = pl.ds(pl.multiple_of((me * held + h) * DK, DK), DK)
         return pltpu.make_async_remote_copy(
-            src_ref=outs.at[a, to],
-            dst_ref=outputs[a].at[:, lanes],
-            send_sem=out_send.at[step, a],
-            recv_sem=out_recv.at[step, a],
+            src_ref=outs.at[a, h, to],
+            dst_ref=out_ref.at[a, :, lanes],
+            send_sem=out_send.at[step, h, a],
+            recv_sem=out_recv.at[step, h, a],
             device_id={"mem": to},
             device_id_type=MESH,
         )
 
-    def finish(step, carry):
-        c = lax.rem(me + 1 + step, groups)
-        for h in range(held):
+    def staying(h, a):
+        lanes = pl.ds(pl.multiple_of((me * held + h) * DK, DK), DK)
+        return pltpu.make_async_copy(outs.at[a, h, me], out_ref.at[a, :, lanes], stay_sem.at[h, a])
+
+    def finish(h):
+        for step in range(groups):
+            c = lax.rem(me + 1 + step, groups)
             col = cols[c, h]
             past, future = (
                 jnp.concatenate(
@@ -428,24 +423,11 @@
                 grad_q += from_past[:, block(e)] * col[:, count + e : count + e + 1]
                 grad_k += from_future[:, block(e)] * col[:, 2 * count + e : 2 * count + e + 1]
             for a, value in enumerate((out, grad_q, grad_k, grad_v)):
-                outs[a, c, :, block(h)] = value.astype(BF16)
-
-        @pl.when(step < groups - 1)
-        def _():
+                outs[a, h, c] = value.astype(BF16)
             for a in range(4):
-                leaving(step, a).start()
-
-        return carry
-
-    lax.fori_loop(0, groups, finish, 0)
-    lanes = pl.ds(pl.multiple_of(me * width, width), width)
-    own = []
-    for a in range(4):
-        copy = pltpu.make_async_copy(outs.at[a, me], outputs[a].at[:, lanes], own_sem.at[0, a])
-        copy.start()
-        own.append(copy)
-    for copy in own:
-        copy.wait()
+                (leaving(step, h, a) if step < groups - 1 else staying(h, a)).start()
+
+    lax.fori_loop(0, held + n_o - 1 + n_i - 1, slot, 0)
 
     def drain(h, carry):
         for a in range(4):
@@ -457,12 +439,13 @@
             def _():
                 hop(w, kind, h, axis, to).wait_send()
 
+        for a in range(4):
+            staying(h, a).wait()
+            for step in range(groups - 1):
+                leaving(step, h, a).wait()
         return carry
 
     lax.fori_loop(0, held, drain, 0)
-    for step in range(groups - 1):
-        for a in range(4):
-            leaving(step, a).wait()
 
 
 def body(queries, keys, values, log_decay, routes, route_logits, cotangent):
@@ -485,18 +468,18 @@
     )
     any_spec = pl.BlockSpec(memory_space=pl.ANY)
     state = (held, DK, count * DK)
-    result = jax.ShapeDtypeStruct((span, features), BF16)
+    result = jax.ShapeDtypeStruct((4, span, features), BF16)
     dma = pltpu.SemaphoreType.DMA
     results = pl.pallas_call(
         functools.partial(kernel, groups, n_i, n_o, held, count),
-        out_shape=[result] * 4,
+        out_shape=result,
         in_specs=[any_spec] * 5,
-        out_specs=[any_spec] * 4,
+        out_specs=any_spec,
         scratch_shapes=[
             pltpu.VMEM((4, held, groups, span, DK), BF16),
             pltpu.VMEM((groups, held, 32, span), F32),
             pltpu.VMEM((groups, held, span, 16), F32),
-            pltpu.VMEM((4, groups, span, held * DK), BF16),
+            pltpu.VMEM((4, held, groups, span, DK), BF16),
             pltpu.VMEM((4, groups, held, span, DK), F32),
             pltpu.VMEM((groups, held, span, count * DK), BF16),
             pltpu.VMEM((groups, held, span, count * DK), BF16),
@@ -520,9 +503,10 @@
             dma((n_o - 1,)),
             dma((2, 3, held)),
             dma((2, 3, held)),
-            dma((groups - 1, 4)),
-            dma((groups - 1, 4)),
+            dma((groups - 1, held, 4)),
+            dma((groups - 1, held, 4)),
             dma,
+            dma((held, 4)),
             dma((held, 4)),
         ],
         compiler_params=pltpu.CompilerParams(
@@ -534,7 +518,7 @@
             transcendentals=0,
         ),
     )(queries[0], keys[0], values[0], cotangent[0], rows)
-    return tuple(item[None] for item in results)
+    return tuple(results[a : a + 1] for a in range(4))
 
 
 def solution(mesh):

time: 92.7 us -> 76.5 us (0.83)
  Pallas kernels: 82.9 us -> 69 us
  local copies, waits for them, and re-layouts: 8.25 us -> 4.7 us
  other arithmetic: 0.31 us -> 1.65 us
    pallas_call x1, Pallas kernels: 82.9 us -> 69 us  [body(): pl.pallas_call(functools.partial(kernel, groups, n_i, n_o, held, count),...]
    unnamed x19 -> x3, local copies, waits for them, and re-layouts: 7.27 us -> 0.08 us
    slice x0 -> x1, local copies, waits for them, and re-layouts: none -> 2.88 us  [body(): return tuple((results[a:a + 1] for a in range(4)))]
where the time goes in v3:
time: 76.5 us; the launch traced here: 76.2 us
  Pallas kernels  69 us (90%)
  local copies, waits for them, and re-layouts  4.7 us (6%)
  other arithmetic  1.65 us (2%)
    pallas_call x1, Pallas kernels, body(): pl.pallas_call(functools.partial(kernel, groups, n_i, n_o, held, count),...  69 us
    slice x1, local copies, waits for them, and re-layouts, body(): return tuple((results[a:a + 1] for a in range(4)))  2.88 us

profile of v3, /device:TPU:0, one launch (start us, length us, event | category | flops | bytes accessed | tf_op | source)
XLA Modules:
  0.0 76.2 jit_solution(11802643371555188743)
XLA Ops:
  0.6 0.7 bitcast_convert_fusion.3
  1.3 0.8 %slice_bitcast_fusion.1 = (s32[128]{0:T(128)S(1)}, s32[128]{0:T(128)S(1)}) fusion(s32[128,2]{0,1:T(2,128)} %bitcast.26), kind=kLoop, calls=%fused_computation.27 | loop fusion | bytes 2048 | tf_op jit(solution)/shard_map/eq | solution.py:30
  2.1 0.7 bitcast_convert_fusion
  2.8 0.2 fusion.1
  3.0 0.2 exponential_reduce_fusion
  3.1 0.1 multiply_dynamic-update-slice_fusion.3
  3.3 0.1 multiply_dynamic-update-slice_fusion.1
  3.4 0.1 multiply_dynamic-update-slice_fusion
  3.5 0.1 broadcast_dynamic-update-slice_fusion
  3.6 0.8 %copy.12 = f32[16,32,128]{2,1,0:T(8,128)} copy(f32[16,32,128]{2,0,1:T(8,128)S(1)} %constant_dynamic-update-slice_fusion) | data formatting | bytes 524288 | tf_op jit(solution)/shard_map/concatenate | solution.py:41
  4.3 69.0 %shard_map.102 = bf16[4,128,2048]{2,1,0:T(8,128)(2,1)} custom-call(bf16[128,2048]{1,0:T(8,128)(2,1)} %bitcast.27, bf16[128,2048]{1,0:T(8,128)(2,1)} %bitcast.28, bf16[128,2048]{1,0:T(8,128)(2,1)} %bitcast.29, bf16[128,2048]{1,0:T(8,128)(2,1)} %bitcast.30, f32[4,4,32,128]{3,2,1,0:T(8,128)} %bitcast.25), custom_call_target="tpu_custom_call" | custom-call | flops 2415919104 | bytes 4194304 | tf_op jit(solution)/shard_map/pallas_call | solution.py:473
  73.4 2.9 %fusion.6 = (bf16[1,128,2048]{2,1,0:T(8,128)(2,1)}, bf16[1,128,2048]{2,1,0:T(8,128)(2,1)}, bf16[1,128,2048]{2,1,0:T(8,128)(2,1)}, bf16[1,128,2048]{2,1,0:T(8,128)(2,1)}) fusion(bf16[4,128,2048]{2,1,0:T(8,128)(2,1)} %shard_map.102), kind=kLoop, calls=%fused_computation.28 | loop fusion | bytes 4194304 | tf_op jit(solution)/shard_map/slice | solution.py:521
  (8 shorter events, 0.1 us)

commit v4 on v3

--- a/solution.py
+++ b/solution.py
@@ -21,37 +21,37 @@
     )
 
 
-def tables(gates, chosen, logits, groups, memories, scale):
-    heads, span = gates.shape
-    held = heads // groups
-    first = jax.nn.sigmoid(logits[:, 0] - logits[:, 1]).astype(BF16).astype(F32)
-    second = jax.nn.sigmoid(logits[:, 1] - logits[:, 0]).astype(BF16).astype(F32)
-    names = jnp.arange(memories, dtype=jnp.int32)[:, None]
-    hit_first = (chosen[:, 0][None, :] == names).astype(F32)
-    hit_second = (chosen[:, 1][None, :] == names).astype(F32)
-    ones = jnp.ones((1, span), F32)
-    mask = jnp.concatenate([hit_first + hit_second, ones], 0)
-    read = jnp.concatenate([first[None] * hit_first + second[None] * hit_second, ones], 0) * scale
-    rates = gates[:, None, :] * mask[None]
-    upper = (jnp.arange(span)[:, None] <= jnp.arange(span)[None, :]).astype(F32)
-    total = jnp.einsum("het,ts->hes", rates, upper, precision=lax.Precision.HIGHEST)
-    middle = total[:, :, span // 2 : span // 2 + 1]
-    end = total[:, :, -1:]
-    count = memories + 1
-    kinds = jnp.concatenate(
-        [
-            read[None] * jnp.exp(total - middle),
-            read[None] * jnp.exp(total),
-            mask[None] * jnp.exp(end - total),
-            jnp.zeros((heads, 16 - 3 * count, span), F32),
-            mask[None] * jnp.exp(middle - total),
-            jnp.zeros((heads, 8 - count, span), F32),
-            jnp.broadcast_to(jnp.exp(end), total.shape),
-            jnp.zeros((heads, 8 - count, span), F32),
-        ],
-        1,
+def fill_tables(table, route_ref, logit_ref, gate_ref, scale):
+    groups, held, _, span = table.shape
+    heads = groups * held
+    names = lax.broadcasted_iota(jnp.int32, (8, span), 0)
+    logits = logit_ref[...].astype(F32)
+    first = jax.nn.sigmoid(logits[0:1] - logits[1:2]).astype(BF16).astype(F32)
+    second = jax.nn.sigmoid(logits[1:2] - logits[0:1]).astype(BF16).astype(F32)
+    hit_first = (route_ref[0:1, :] == names).astype(F32)
+    hit_second = (route_ref[1:2, :] == names).astype(F32)
+    shared = (names == MEM_DEV * groups).astype(F32)
+    above = lax.broadcasted_iota(jnp.int32, (span, span), 0)
+    along = lax.broadcasted_iota(jnp.int32, (span, span), 1)
+    upper = (above <= along).astype(F32).astype(BF16)
+    mask = hit_first + hit_second + shared
+    read = (first * hit_first + second * hit_second + shared) * scale
+    gates = gate_ref[...].astype(F32)
+    rates = jnp.concatenate([gates[h : h + 1] * mask for h in range(heads)], 0)
+    total = dot(rates.astype(BF16), upper, 1, 0)
+    middle = total[:, span // 2 : span // 2 + 1]
+    end = total[:, span - 1 :]
+    masks = jnp.concatenate([mask] * heads, 0)
+    reads = jnp.concatenate([read] * heads, 0)
+    kinds = (
+        reads * jnp.exp(total - middle),
+        reads * jnp.exp(total),
+        masks * jnp.exp(end - total),
+        masks * jnp.exp(middle - total),
+        jnp.broadcast_to(jnp.exp(end), total.shape),
     )
-    return kinds.reshape(groups, held, 32, span)
+    for n, kind in enumerate(kinds):
+        table[:, :, 8 * n : 8 * n + 8, :] = kind.reshape(groups, held, 8, span)
 
 
 def kernel(
@@ -60,13 +60,17 @@
     n_o,
     held,
     count,
+    scale,
     q_ref,
     k_ref,
     v_ref,
     g_ref,
-    row_ref,
+    route_ref,
+    logit_ref,
+    gate_ref,
     out_ref,
     x,
+    row_ref,
     rows,
     cols,
     outs,
@@ -157,11 +161,6 @@
         lanes = pl.ds(pl.multiple_of((me * held + h) * DK, DK), DK)
         return pltpu.make_async_copy(inputs[a].at[:, lanes], x.at[a, h, me], own_sem.at[h, a])
 
-    for off in range(1, groups):
-        row_copy(off).start()
-    own_rows = pltpu.make_async_copy(row_ref.at[me], rows.at[me], row_sem)
-    own_rows.start()
-
     def start_in(h, carry):
         for a in range(4):
             for off in range(1, groups):
@@ -169,12 +168,20 @@
             own_copy(h, a).start()
         return carry
 
-    lax.fori_loop(0, held, start_in, 0)
+    start_in(0, 0)
+    fill_tables(row_ref, route_ref, logit_ref, gate_ref, scale)
+    for off in range(1, groups):
+        row_copy(off).start()
+    own_rows = pltpu.make_async_copy(row_ref.at[me], rows.at[me], row_sem)
+    own_rows.start()
+    lax.fori_loop(1, held, start_in, 0)
+    for c, local in ((0, local_f), (groups - 1, local_b)):
+        local[c] = jnp.zeros((held, DK, count * DK), F32)
     own_rows.wait()
     for off in range(1, groups):
         row_copy(off).wait()
 
-    chunk_decay = [rows[c, :, 24:32, :] for c in range(groups)]
+    chunk_decay = [rows[c, :, 32:40, :] for c in range(groups)]
     total = jnp.ones((held, 8, span), F32)
     for c in range(groups):
         near_f[c] = total
@@ -201,12 +208,10 @@
         return slice(e * DK, (e + 1) * DK)
 
     def gather_states(h):
-        run_f[h] = jnp.zeros((DK, count * DK), F32)
-        run_b[h] = jnp.zeros((DK, count * DK), F32)
         for c in range(groups):
-            col = rows[c, h, 0:16, :].T
+            col = rows[c, h, 0:24, :].T
             cols[c, h] = col
-            for a, saved, first in ((1, kbs, 2 * count), (0, qas, count)):
+            for a, saved, first in ((1, kbs, 16), (0, qas, 8)):
                 value = x[a, h, c].astype(F32)
                 saved[c, h] = jnp.concatenate(
                     [
@@ -215,16 +220,18 @@
                     ],
                     1,
                 )
-        for step in range(groups):
-            for c, a, saved, run, local in (
-                (step, 2, kbs, run_f, local_f),
-                (groups - 1 - step, 3, qas, run_b, local_b),
-            ):
-                state = dot(x[a, h, c], saved[c, h], 0, 0)
-                for e in range(count):
-                    old = run[h, :, block(e)]
-                    local[c, h, :, block(e)] = old
-                    run[h, :, block(e)] = old * rows[c, h, 24 + e : 25 + e, :] + state[:, block(e)]
+        forward = list(range(groups))
+        for order, a, saved, run, local in (
+            (forward, 2, kbs, run_f, local_f),
+            (forward[::-1], 3, qas, run_b, local_b),
+        ):
+            states = [dot(x[a, h, c], saved[c, h], 0, 0) for c in order]
+            for e in range(count):
+                total = states[0][:, block(e)]
+                for c, state in zip(order[1:], states[1:]):
+                    local[c, h, :, block(e)] = total
+                    total = total * rows[c, h, 32 + e : 33 + e, :] + state[:, block(e)]
+                run[h, :, block(e)] = total
 
     lower = lax.broadcasted_iota(jnp.int32, (span, span), 0) >= lax.broadcasted_iota(
         jnp.int32, (span, span), 1
@@ -236,7 +243,7 @@
             col = cols[c, h]
             weight = jnp.zeros((span, span), F32)
             for e in range(count):
-                weight += col[:, e : e + 1] * rows[c, h, 16 + e : 17 + e, :]
+                weight += col[:, e : e + 1] * rows[c, h, 24 + e : 25 + e, :]
             weight = jnp.where(lower, weight, 0.0)
             sw = (dot(q, k, 1, 1) * weight).astype(BF16)
             gw = (dot(g, v, 1, 1) * weight).astype(BF16)
@@ -420,12 +427,14 @@
             from_past = dot(x[3, h, c], past, 1, 0)
             from_future = dot(x[2, h, c], future, 1, 0)
             for e in range(count):
-                grad_q += from_past[:, block(e)] * col[:, count + e : count + e + 1]
-                grad_k += from_future[:, block(e)] * col[:, 2 * count + e : 2 * count + e + 1]
+                grad_q += from_past[:, block(e)] * col[:, 8 + e : 9 + e]
+                grad_k += from_future[:, block(e)] * col[:, 16 + e : 17 + e]
             for a, value in enumerate((out, grad_q, grad_k, grad_v)):
                 outs[a, h, c] = value.astype(BF16)
-            for a in range(4):
-                (leaving(step, h, a) if step < groups - 1 else staying(h, a)).start()
+            if step % 2 == 1 or step == groups - 1:
+                for one in range(step - step % 2, step + 1):
+                    for a in range(4):
+                        (leaving(one, h, a) if one < groups - 1 else staying(h, a)).start()
 
     lax.fori_loop(0, held + n_o - 1 + n_i - 1, slot, 0)
 
@@ -458,27 +467,20 @@
     held = heads // groups
     count = memories + 1
     scale = 2.0 / math.sqrt(DK * span * groups * n_i * n_o)
-    rows = tables(
-        log_decay[:, 0, :].astype(F32),
-        routes[0],
-        route_logits[0].astype(F32),
-        groups,
-        memories,
-        scale,
-    )
     any_spec = pl.BlockSpec(memory_space=pl.ANY)
     state = (held, DK, count * DK)
     result = jax.ShapeDtypeStruct((4, span, features), BF16)
     dma = pltpu.SemaphoreType.DMA
     results = pl.pallas_call(
-        functools.partial(kernel, groups, n_i, n_o, held, count),
+        functools.partial(kernel, groups, n_i, n_o, held, count, scale),
         out_shape=result,
-        in_specs=[any_spec] * 5,
+        in_specs=[any_spec] * 4 + [pl.BlockSpec(memory_space=pltpu.VMEM)] * 3,
         out_specs=any_spec,
         scratch_shapes=[
             pltpu.VMEM((4, held, groups, span, DK), BF16),
-            pltpu.VMEM((groups, held, 32, span), F32),
-            pltpu.VMEM((groups, held, span, 16), F32),
+            pltpu.VMEM((groups, held, 40, span), F32),
+            pltpu.VMEM((groups, held, 40, span), F32),
+            pltpu.VMEM((groups, held, span, 24), F32),
             pltpu.VMEM((4, held, groups, span, DK), BF16),
             pltpu.VMEM((4, groups, held, span, DK), F32),
             pltpu.VMEM((groups, held, span, count * DK), BF16),
@@ -517,7 +519,7 @@
             bytes_accessed=16 * span * features,
             transcendentals=0,
         ),
-    )(queries[0], keys[0], values[0], cotangent[0], rows)
+    )(queries[0], keys[0], values[0], cotangent[0], routes[0].T, route_logits[0].T, log_decay[:, 0])
     return tuple(results[a : a + 1] for a in range(4))
 
 

time: 76.5 us -> 77.2 us (level)
  Pallas kernels: 69 us -> 73.5 us
  local copies, waits for them, and re-layouts: 4.7 us -> 2.88 us
  other arithmetic: 1.65 us -> 0 us
    pallas_call x1, Pallas kernels: 69 us -> 73.5 us  [body(): pl.pallas_call(functools.partial(kernel, groups, n_i, n_o, held, count, s...]
    concatenate x3 -> x0, local copies, waits for them, and re-layouts: 0.8 us -> none  [the longest x2 0.79 us: tables(): jnp.concatenate([read[None] * jnp.exp(total - middle), read[None] * jnp.e...]
where the time goes in v4:
time: 77.2 us; the launch traced here: 77 us
  Pallas kernels  73.5 us (95%)
  local copies, waits for them, and re-layouts  2.88 us (4%)
    pallas_call x1, Pallas kernels, body(): pl.pallas_call(functools.partial(kernel, groups, n_i, n_o, held, count, s...  73.5 us
    slice x1, local copies, waits for them, and re-layouts, body(): return tuple((results[a:a + 1] for a in range(4)))  2.88 us

profile of v4, /device:TPU:0, one launch (start us, length us, event | category | flops | bytes accessed | tf_op | source)
XLA Modules:
  0.0 77.0 jit_solution(18034310236833698204)
XLA Ops:
  0.6 73.5 %shard_map.102 = bf16[4,128,2048]{2,1,0:T(8,128)(2,1)} custom-call(bf16[128,2048]{1,0:T(8,128)(2,1)} %bitcast.11, bf16[128,2048]{1,0:T(8,128)(2,1)} %bitcast.12, bf16[128,2048]{1,0:T(8,128)(2,1)} %bitcast.13, bf16[128,2048]{1,0:T(8,128)(2,1)} %bitcast.14, s32[2,128]{1,0:T(2,128)} %bitcast.16, bf16[2,128]{1,0:T(2,128)(2,1)} %bitcast.17, bf16[16,128]{1,0:T(8,128)(2,1)} %bitcast.15), custom_call_target="tpu_custom_call" | custom-call | flops 2415919104 | bytes 4194304 | tf_op jit(solution)/shard_map/pallas_call | solution.py:474
  74.2 2.9 %fusion = (bf16[1,128,2048]{2,1,0:T(8,128)(2,1)}, bf16[1,128,2048]{2,1,0:T(8,128)(2,1)}, bf16[1,128,2048]{2,1,0:T(8,128)(2,1)}, bf16[1,128,2048]{2,1,0:T(8,128)(2,1)}) fusion(bf16[4,128,2048]{2,1,0:T(8,128)(2,1)} %shard_map.102), kind=kLoop, calls=%fused_computation | loop fusion | bytes 4194304 | tf_op jit(solution)/shard_map/slice | solution.py:523

commit v5 on v4

--- a/solution.py
+++ b/solution.py
@@ -10,6 +10,7 @@
 
 DK = 128
 MEM_DEV = 1
+STRIDE = 2
 MESH = pl.DeviceIdType.MESH
 F32 = jnp.float32
 BF16 = jnp.bfloat16
@@ -132,6 +133,9 @@
         )
 
     sides = jnp.where(i > 0, 1, 0) + jnp.where(i < n_i - 1, 1, 0)
+    fill_tables(row_ref, route_ref, logit_ref, gate_ref, scale)
+    for c, local in ((0, local_f), (groups - 1, local_b)):
+        local[c] = jnp.zeros((held, DK, count * DK), F32)
     pl.semaphore_wait(barrier, groups - 1 + n_o - 1 + sides)
 
     def row_copy(off):
@@ -168,15 +172,11 @@
             own_copy(h, a).start()
         return carry
 
-    start_in(0, 0)
-    fill_tables(row_ref, route_ref, logit_ref, gate_ref, scale)
     for off in range(1, groups):
         row_copy(off).start()
     own_rows = pltpu.make_async_copy(row_ref.at[me], rows.at[me], row_sem)
     own_rows.start()
-    lax.fori_loop(1, held, start_in, 0)
-    for c, local in ((0, local_f), (groups - 1, local_b)):
-        local[c] = jnp.zeros((held, DK, count * DK), F32)
+    lax.fori_loop(0, held, start_in, 0)
     own_rows.wait()
     for off in range(1, groups):
         row_copy(off).wait()
@@ -321,13 +321,24 @@
         send(w, 1, h)
 
     def slot(t, carry):
-        @pl.when(t < held)
-        def _():
+        def step(lag, *work):
+            since = t - lag
+            h = lax.div(since, STRIDE)
+            now = jnp.logical_and(since >= 0, lax.rem(since, STRIDE) == 0)
+
+            @pl.when(jnp.logical_and(now, h < held))
+            def _():
+                for one in work:
+                    one(h)
+
+        def enter_block(h):
             for a in range(4):
-                own_copy(t, a).wait()
+                own_copy(h, a).wait()
                 for off in range(1, groups):
-                    in_copy(off, t, a).wait_recv()
-            gather_states(t)
+                    in_copy(off, h, a).wait_recv()
+            gather_states(h)
+
+        step(0, enter_block)
 
         @pl.when(t == 0)
         def _():
@@ -344,36 +355,12 @@
             derived[2] = block_decay[o]
             derived[3] = before * later * block_decay[o]
 
-        rising = t - o
-        falling = t - (n_o - 1 - o)
-
-        @pl.when(jnp.logical_and(rising >= 0, rising < held))
-        def _():
-            prefix(0, rising)
-            rest(1, rising)
-
-        @pl.when(jnp.logical_and(falling >= 0, falling < held))
-        def _():
-            prefix(1, falling)
-            rest(0, falling)
-
-        @pl.when(t < held)
-        def _():
-            within(t)
-
+        step(o, functools.partial(prefix, 0), functools.partial(rest, 1))
+        step(n_o - 1 - o, functools.partial(prefix, 1), functools.partial(rest, 0))
         for w, place in ((0, i), (1, n_i - 1 - i)):
-            crossing = t - (n_o - 1) - place
-
-            @pl.when(jnp.logical_and(crossing >= 0, crossing < held))
-            def _():
-                entering(w, crossing)
-
-        done = t - (n_o - 1) - (n_i - 1)
-
-        @pl.when(done >= 0)
-        def _():
-            finish(done)
-
+            step(n_o - 1 + place, functools.partial(entering, w))
+        step(1, within)
+        step(n_o - 1 + n_i - 1, finish)
         return carry
 
     def entering(w, h):
@@ -436,7 +423,7 @@
                     for a in range(4):
                         (leaving(one, h, a) if one < groups - 1 else staying(h, a)).start()
 
-    lax.fori_loop(0, held + n_o - 1 + n_i - 1, slot, 0)
+    lax.fori_loop(0, STRIDE * (held - 1) + n_o + n_i - 1, slot, 0)
 
     def drain(h, carry):
         for a in range(4):

time: 77.2 us -> 77.1 us (level)
  no operation moved by 1% of the time
where the time goes in v5:
time: 77.1 us; the launch traced here: 76.9 us
  Pallas kernels  73.4 us (95%)
  local copies, waits for them, and re-layouts  2.88 us (4%)
    pallas_call x1, Pallas kernels, body(): pl.pallas_call(functools.partial(kernel, groups, n_i, n_o, held, count, s...  73.4 us
    slice x1, local copies, waits for them, and re-layouts, body(): return tuple((results[a:a + 1] for a in range(4)))  2.88 us

profile of v5, /device:TPU:0, one launch (start us, length us, event | category | flops | bytes accessed | tf_op | source)
XLA Modules:
  0.0 76.9 jit_solution(1607738817738604228)
XLA Ops:
  0.6 73.4 %shard_map.102 = bf16[4,128,2048]{2,1,0:T(8,128)(2,1)} custom-call(bf16[128,2048]{1,0:T(8,128)(2,1)} %bitcast.11, bf16[128,2048]{1,0:T(8,128)(2,1)} %bitcast.12, bf16[128,2048]{1,0:T(8,128)(2,1)} %bitcast.13, bf16[128,2048]{1,0:T(8,128)(2,1)} %bitcast.14, s32[2,128]{1,0:T(2,128)} %bitcast.16, bf16[2,128]{1,0:T(2,128)(2,1)} %bitcast.17, bf16[16,128]{1,0:T(8,128)(2,1)} %bitcast.15), custom_call_target="tpu_custom_call" | custom-call | flops 2415919104 | bytes 4194304 | tf_op jit(solution)/shard_map/pallas_call | solution.py:461
  74.1 2.9 %fusion = (bf16[1,128,2048]{2,1,0:T(8,128)(2,1)}, bf16[1,128,2048]{2,1,0:T(8,128)(2,1)}, bf16[1,128,2048]{2,1,0:T(8,128)(2,1)}, bf16[1,128,2048]{2,1,0:T(8,128)(2,1)}) fusion(bf16[4,128,2048]{2,1,0:T(8,128)(2,1)} %shard_map.102), kind=kLoop, calls=%fused_computation | loop fusion | bytes 4194304 | tf_op jit(solution)/shard_map/slice | solution.py:510

commit v6 on v5

--- a/solution.py
+++ b/solution.py
@@ -10,7 +10,7 @@
 
 DK = 128
 MEM_DEV = 1
-STRIDE = 2
+STRIDE = 1
 MESH = pl.DeviceIdType.MESH
 F32 = jnp.float32
 BF16 = jnp.bfloat16

time: 77.1 us -> 74.1 us (0.961)
  Pallas kernels: 73.4 us -> 70.4 us
    pallas_call x1, Pallas kernels: 73.4 us -> 70.4 us  [body(): pl.pallas_call(functools.partial(kernel, groups, n_i, n_o, held, count, s...]
where the time goes in v6:
time: 74.1 us; the launch traced here: 73.9 us
  Pallas kernels  70.4 us (95%)
  local copies, waits for them, and re-layouts  2.88 us (4%)
    pallas_call x1, Pallas kernels, body(): pl.pallas_call(functools.partial(kernel, groups, n_i, n_o, held, count, s...  70.4 us
    slice x1, local copies, waits for them, and re-layouts, body(): return tuple((results[a:a + 1] for a in range(4)))  2.88 us

profile of v6, /device:TPU:0, one launch (start us, length us, event | category | flops | bytes accessed | tf_op | source)
XLA Modules:
  0.0 73.9 jit_solution(13066884820717859863)
XLA Ops:
  0.6 70.4 %shard_map.102 = bf16[4,128,2048]{2,1,0:T(8,128)(2,1)} custom-call(bf16[128,2048]{1,0:T(8,128)(2,1)} %bitcast.11, bf16[128,2048]{1,0:T(8,128)(2,1)} %bitcast.12, bf16[128,2048]{1,0:T(8,128)(2,1)} %bitcast.13, bf16[128,2048]{1,0:T(8,128)(2,1)} %bitcast.14, s32[2,128]{1,0:T(2,128)} %bitcast.16, bf16[2,128]{1,0:T(2,128)(2,1)} %bitcast.17, bf16[16,128]{1,0:T(8,128)(2,1)} %bitcast.15), custom_call_target="tpu_custom_call" | custom-call | flops 2415919104 | bytes 4194304 | tf_op jit(solution)/shard_map/pallas_call | solution.py:461
  71.0 2.9 %fusion = (bf16[1,128,2048]{2,1,0:T(8,128)(2,1)}, bf16[1,128,2048]{2,1,0:T(8,128)(2,1)}, bf16[1,128,2048]{2,1,0:T(8,128)(2,1)}, bf16[1,128,2048]{2,1,0:T(8,128)(2,1)}) fusion(bf16[4,128,2048]{2,1,0:T(8,128)(2,1)} %shard_map.102), kind=kLoop, calls=%fused_computation | loop fusion | bytes 4194304 | tf_op jit(solution)/shard_map/slice | solution.py:510
